TPU v7x, 32 devices: a whole 2x2x4 slice. The times are simulated.
32 devices in a mesh: section: 2 (over core), dp: 8 (over z, y), tensor: 2 (over x).
Axes of the slice: x: 2, y: 2, z: 4, core: 2. Of those that a mesh axis runs over, the one named last changes fastest.
Arguments:
- inputs: bfloat16 [16, 512, 768], P('dp'), may hold values from -6 to 6
- segments: int32 [16, 512], P('dp'), may hold values from 0 to 15, never falling along the last dimension, each value on 1 to 64 neighbouring positions
- partner: int32 [16, 16], P('dp'), may hold values from 0 to 15, as said below
- grad_output: bfloat16 [16, 512, 768], P('dp'), may hold values from -6 to 6
- w_qkv: bfloat16 [2, 768, 3, 768], P('section', 'dp', None, 'tensor'), may hold values from -0.21875 to 0.21875
- w_out: bfloat16 [2, 768, 768], P('section', 'tensor', 'dp'), may hold values from -0.875 to 0.875
- w_up: bfloat16 [2, 768, 3072], P('section', 'dp', 'tensor'), may hold values from -0.21875 to 0.21875
- w_down: bfloat16 [2, 3072, 768], P('section', 'tensor', 'dp'), may hold values from -0.109375 to 0.109375
- norm_gain: bfloat16 [2, 2, 768], P('section', None, 'dp'), may hold values from 0.25 to 1.75
- norm_shift: bfloat16 [2, 2, 768], P('section', None, 'dp'), may hold values from -3 to 3
Outputs:
- layer_outputs: bfloat16 [2, 16, 512, 768], P('section', 'dp')
- input_grads: bfloat16 [2, 16, 512, 768], P('section', 'dp')
- grad_qkv: float32 [2, 768, 3, 768], P('section', 'dp', None, 'tensor')
- grad_out: float32 [2, 768, 768], P('section', 'tensor', 'dp')
- grad_up: float32 [2, 768, 3072], P('section', 'dp', 'tensor')
- grad_down: float32 [2, 3072, 768], P('section', 'tensor', 'dp')
- grad_gain: float32 [2, 2, 768], P('section', None, 'dp')
- grad_shift: float32 [2, 2, 768], P('section', None, 'dp')
Inputs may be any that keep to these rules, and one draw needn't show every extreme that they name: partner pairs the segments of a row: an even segment maps to an odd one and back, and partner of partner is the segment itself. Each row holds all 16 segments in order, of 1 to 64 tokens, at least one of exactly 64.
All inputs are finite; a program needn't handle non-finite values.
Results may differ from a plain program's by a relative error of at most 0.028.
Values may be sent and summed in bfloat16 or wider, within the bound.
A program may use at most 192 MiB of HBM per device.

v0:
```python
import jax
import jax.numpy as jnp
from jax import lax
from jax.sharding import PartitionSpec as P

HEAD = 64
MICRO = 2


norm_eps = 1e-06
score_scale = 0.125
masked_value = -1000000000.0


def shifted(shard, axis, by):
    peers = lax.axis_size(axis)
    pairs = [(i, i + by) for i in range(peers) if 0 <= i + by < peers]
    return lax.ppermute(shard, axis, pairs)


def partner_of(segment_ids, partner):
    table = jnp.arange(partner.shape[-1], dtype=jnp.int32)
    hits = segment_ids[..., None] == table
    return jnp.sum(jnp.where(hits, partner[:, None, :], 0), -1)


def layer_norm(values, gain, shift):
    center = values - jnp.mean(values, -1, keepdims=True)
    inverse = lax.rsqrt(jnp.mean(center * center, -1, keepdims=True) + norm_eps)
    normed = center * inverse
    return (normed * gain + shift, normed, inverse)


def norm_back(grad, normed, inverse, gain):
    scaled = grad * gain
    inner = (
        scaled
        - jnp.mean(scaled, -1, keepdims=True)
        - normed * jnp.mean(scaled * normed, -1, keepdims=True)
    )
    return inner * inverse


def gelu_slope(values):
    lower = 0.5 * (1.0 + lax.erf(values * 0.7071067811865476))
    density = jnp.exp(-0.5 * values * values) * 0.3989422804014327
    return lower + values * density


def tensor_sum(partial_value):
    return lax.psum(partial_value.astype(jnp.bfloat16), "tensor").astype(jnp.float32)


def back_sum(partial_value):
    return lax.psum(partial_value.astype(jnp.bfloat16), "tensor").astype(jnp.float32)


def masked_scores(query, key, query_groups, key_groups):
    scores = (
        jnp.einsum("qhd,khd->hqk", query, key, preferred_element_type=jnp.float32) * score_scale
    )
    allowed = query_groups[:, None] == key_groups[None, :]
    return jnp.where(allowed[None], scores, masked_value)


def attend(query, key, value, query_groups, key_groups):
    scores = masked_scores(query, key, query_groups, key_groups)
    top = jnp.max(scores, -1, keepdims=True)
    expo = jnp.exp(scores - top)
    total = jnp.sum(expo, -1, keepdims=True)
    probs = (expo / total).astype(jnp.bfloat16)
    mixed = jnp.einsum("hqk,khd->qhd", probs, value, preferred_element_type=jnp.float32)
    return (mixed.astype(jnp.bfloat16), (top + jnp.log(total))[..., 0])


def attend_back(query, key, value, query_groups, key_groups, spread, grad_mixed):
    scores = masked_scores(query, key, query_groups, key_groups)
    probs = jnp.exp(scores - spread[..., None])
    probs_low = probs.astype(jnp.bfloat16)
    grad_probs = jnp.einsum("qhd,khd->hqk", grad_mixed, value, preferred_element_type=jnp.float32)
    grad_value = jnp.einsum(
        "hqk,qhd->khd", probs_low, grad_mixed, preferred_element_type=jnp.float32
    )
    row_dot = jnp.sum(probs * grad_probs, -1, keepdims=True)
    grad_scores = (probs * (grad_probs - row_dot)).astype(jnp.bfloat16)
    grad_query = (
        jnp.einsum("hqk,khd->qhd", grad_scores, key, preferred_element_type=jnp.float32)
        * score_scale
    )
    grad_key = (
        jnp.einsum("hqk,qhd->khd", grad_scores, query, preferred_element_type=jnp.float32)
        * score_scale
    )
    return jnp.stack(
        [
            grad_query.astype(jnp.bfloat16),
            grad_key.astype(jnp.bfloat16),
            grad_value.astype(jnp.bfloat16),
        ],
        1,
    )


def layer_forward(inputs, weights, query_groups, key_groups):
    w_qkv, w_out, w_up, w_down, gains, shifts = weights
    rows, length, width = inputs.shape
    local = w_qkv.shape[2]
    flat = inputs.reshape(rows * length, width)
    packed = jnp.einsum("nd,dcm->ncm", flat, w_qkv, preferred_element_type=jnp.float32).astype(
        jnp.bfloat16
    )
    heads = packed.reshape(rows, length, 3, local // HEAD, HEAD)
    mixed, spread = lax.map(
        lambda item: attend(*item),
        (heads[:, :, 0], heads[:, :, 1], heads[:, :, 2], query_groups, key_groups),
    )
    mixed_flat = mixed.reshape(rows * length, local)
    flat_wide = flat.astype(jnp.float32)
    attn_out = tensor_sum(jnp.dot(mixed_flat, w_out, preferred_element_type=jnp.float32))
    hidden, normed_first, inverse_first = layer_norm(
        flat_wide + attn_out, gains[0].astype(jnp.float32), shifts[0].astype(jnp.float32)
    )
    hidden_low = hidden.astype(jnp.bfloat16)
    pre = jnp.dot(hidden_low, w_up, preferred_element_type=jnp.float32)
    act = jax.nn.gelu(pre, approximate=False).astype(jnp.bfloat16)
    ffn_out = tensor_sum(jnp.dot(act, w_down, preferred_element_type=jnp.float32))
    result, normed_second, inverse_second = layer_norm(
        hidden + ffn_out, gains[1].astype(jnp.float32), shifts[1].astype(jnp.float32)
    )
    result_low = result.astype(jnp.bfloat16)
    kept = (
        flat,
        heads,
        spread,
        mixed_flat,
        normed_first,
        inverse_first,
        hidden_low,
        pre,
        act,
        normed_second,
        inverse_second,
    )
    return (result_low.reshape(rows, length, width), kept)


def layer_backward(grad_result, kept, weights, query_groups, key_groups):
    w_qkv, w_out, w_up, w_down, gains, shifts = weights
    (
        flat,
        heads,
        spread,
        mixed_flat,
        normed_first,
        inverse_first,
        hidden_low,
        pre,
        act,
        normed_second,
        inverse_second,
    ) = kept
    rows, length, width = (heads.shape[0], heads.shape[1], flat.shape[1])
    local = w_qkv.shape[2]
    gain_second = jnp.sum(grad_result * normed_second, 0)
    shift_second = jnp.sum(grad_result, 0)
    grad_sum2 = norm_back(grad_result, normed_second, inverse_second, gains[1].astype(jnp.float32))
    grad_ffn = grad_sum2.astype(jnp.bfloat16)
    grad_down = jnp.einsum("nf,nd->fd", act, grad_ffn, preferred_element_type=jnp.float32)
    grad_act = jnp.einsum("nd,fd->nf", grad_ffn, w_down, preferred_element_type=jnp.float32)
    grad_pre = (grad_act * gelu_slope(pre)).astype(jnp.bfloat16)
    grad_up = jnp.einsum("nd,nf->df", hidden_low, grad_pre, preferred_element_type=jnp.float32)
    grad_hidden = grad_sum2 + back_sum(
        jnp.einsum("nf,df->nd", grad_pre, w_up, preferred_element_type=jnp.float32)
    )
    gain_first = jnp.sum(grad_hidden * normed_first, 0)
    shift_first = jnp.sum(grad_hidden, 0)
    grad_resid = norm_back(grad_hidden, normed_first, inverse_first, gains[0].astype(jnp.float32))
    grad_attn = grad_resid.astype(jnp.bfloat16)
    grad_out = jnp.einsum("nm,nd->md", mixed_flat, grad_attn, preferred_element_type=jnp.float32)
    grad_mixed = jnp.einsum(
        "nd,md->nm", grad_attn, w_out, preferred_element_type=jnp.float32
    ).astype(jnp.bfloat16)
    grad_mixed = grad_mixed.reshape(rows, length, local // HEAD, HEAD)
    grad_heads = lax.map(
        lambda item: attend_back(*item),
        (
            heads[:, :, 0],
            heads[:, :, 1],
            heads[:, :, 2],
            query_groups,
            key_groups,
            spread,
            grad_mixed,
        ),
    )
    grad_packed = grad_heads.reshape(rows * length, 3, local)
    grad_qkv = jnp.einsum("nd,ncm->dcm", flat, grad_packed, preferred_element_type=jnp.float32)
    grad_input = grad_resid + back_sum(
        jnp.einsum("ncm,dcm->nd", grad_packed, w_qkv, preferred_element_type=jnp.float32)
    )
    grad_low = grad_input.astype(jnp.bfloat16)
    grads = (
        grad_qkv,
        grad_out,
        grad_up,
        grad_down,
        jnp.stack([gain_first, gain_second]),
        jnp.stack([shift_first, shift_second]),
    )
    return (grads, grad_low.reshape(rows, length, width))


def shards(
    inputs, segments, partner, grad_output, w_qkv, w_out, w_up, w_down, norm_gain, norm_shift
):
    phase = lax.axis_index("section")
    rows = inputs.shape[0] // MICRO
    length, width = (inputs.shape[1], inputs.shape[2])
    weights = (
        lax.all_gather(w_qkv[0], "dp", axis=0, tiled=True),
        lax.all_gather(w_out[0], "dp", axis=1, tiled=True),
        lax.all_gather(w_up[0], "dp", axis=0, tiled=True),
        lax.all_gather(w_down[0], "dp", axis=1, tiled=True),
        lax.all_gather(norm_gain[0], "dp", axis=1, tiled=True),
        lax.all_gather(norm_shift[0], "dp", axis=1, tiled=True),
    )
    mapped = partner_of(segments, partner)
    query_all = jnp.where(phase == 0, segments, mapped)
    received = jnp.zeros((rows, length, width), jnp.bfloat16)
    saved_ticks = []
    results = []
    for tick in range(MICRO + 1):
        start = jnp.clip(tick - phase, 0, MICRO - 1) * rows
        own = lax.dynamic_slice_in_dim(inputs, start, rows, 0)
        layer_in = jnp.where(phase == 0, own, received)
        query_groups = lax.dynamic_slice_in_dim(query_all, start, rows, 0)
        key_groups = lax.dynamic_slice_in_dim(segments, start, rows, 0)
        result, unused = layer_forward(layer_in, weights, query_groups, key_groups)
        saved_ticks.append((layer_in, query_groups, key_groups))
        results.append(result)
        if tick < MICRO:
            received = shifted(result, "section", 1)
    grad_received = jnp.zeros((rows, length, width), jnp.bfloat16)
    totals = None
    grad_inputs = []
    for tick in range(MICRO + 1):
        micro_index = MICRO - tick - phase
        valid = (micro_index >= 0) & (micro_index < MICRO)
        start = jnp.clip(micro_index, 0, MICRO - 1) * rows
        layer_in, query_groups, key_groups = saved_ticks[MICRO - tick]
        unused, kept = layer_forward(layer_in, weights, query_groups, key_groups)
        own_grad = lax.dynamic_slice_in_dim(grad_output, start, rows, 0)
        grad_in = (
            jnp.where(phase == 1, own_grad, grad_received)
            .astype(jnp.float32)
            .reshape(rows * length, width)
        )
        grads, grad_low = layer_backward(grad_in, kept, weights, query_groups, key_groups)
        grads = jax.tree.map(lambda value: jnp.where(valid, value, 0.0), grads)
        totals = (
            grads
            if totals is None
            else jax.tree.map(lambda left, right: left + right, totals, grads)
        )
        grad_inputs.append(grad_low)
        if tick < MICRO:
            grad_received = shifted(grad_low, "section", -1)
    totals = (
        lax.psum_scatter(totals[0], "dp", scatter_dimension=0, tiled=True),
        lax.psum_scatter(totals[1], "dp", scatter_dimension=1, tiled=True),
        lax.psum_scatter(totals[2], "dp", scatter_dimension=0, tiled=True),
        lax.psum_scatter(totals[3], "dp", scatter_dimension=1, tiled=True),
        lax.psum_scatter(totals[4], "dp", scatter_dimension=1, tiled=True),
        lax.psum_scatter(totals[5], "dp", scatter_dimension=1, tiled=True),
    )
    result_stack = jnp.stack(results)
    layer_outputs = lax.dynamic_slice_in_dim(result_stack, phase, MICRO, 0).reshape(
        MICRO * rows, length, width
    )
    grad_stack = jnp.stack(grad_inputs[::-1])
    input_grads = lax.dynamic_slice_in_dim(grad_stack, phase, MICRO, 0).reshape(
        MICRO * rows, length, width
    )
    grad_qkv, grad_out, grad_up, grad_down, grad_gain, grad_shift = totals
    return (
        layer_outputs[None],
        input_grads[None],
        grad_qkv[None],
        grad_out[None],
        grad_up[None],
        grad_down[None],
        grad_gain[None],
        grad_shift[None],
    )


def solution(mesh):
    placed = (
        P("dp", None, None),
        P("dp", None),
        P("dp", None),
        P("dp", None, None),
        P("section", "dp", None, "tensor"),
        P("section", "tensor", "dp"),
        P("section", "dp", "tensor"),
        P("section", "tensor", "dp"),
        P("section", None, "dp"),
        P("section", None, "dp"),
    )
    return jax.shard_map(
        shards,
        mesh=mesh,
        in_specs=placed,
        out_specs=(
            P("section", "dp", None, None),
            P("section", "dp", None, None),
            P("section", "dp", None, "tensor"),
            P("section", "tensor", "dp"),
            P("section", "dp", "tensor"),
            P("section", "tensor", "dp"),
            P("section", None, "dp"),
            P("section", None, "dp"),
        ),
        check_vma=False,
    )
```

profile of v0, /device:TPU:0, one launch (start us, length us, event | category | flops | bytes accessed | tf_op | source)
XLA Modules:
  0.0 1251.7 jit_solution(7107680810995356839)
XLA Ops:
  10.5 34.1 %all-gather.1 = bf16[1,384,768]{1,2,0:T(8,128)(2,1)S(1)} all-gather(bf16[1,384,96]{1,2,0:T(8,128)(2,1)} %param.15), channel_id=3, replica_groups=mesh['section'=2,'dp'=8,'tensor'=2] {'dp'}, dimensions={2}, use_global_device_ids=true | all-gather | bytes 663552 | tf_op jit(solution)/shard_map/all_gather | solution.py:221
  44.6 15.7 %all-gather.10.cloned.1.call-done = bf16[1,768,3,384]{3,1,2,0:T(8,128)(2,1)} async-done(((bf16[1,96,3,384]{3,1,2,0:T(8,128)(2,1)}), bf16[1,768,3,384]{3,1,2,0:T(8,128)(2,1)}) %all-gather.10.cloned.1.call-update) | async-done | bytes 1769488 | tf_op jit(solution)/shard_map/all_gather | solution.py:220
  72.2 31.0 %all-gather.2 = bf16[1,2,768]{1,0,2:T(2,128)(2,1)S(1)} all-gather(bf16[1,2,96]{1,0,2:T(2,128)(2,1)S(1)} %copy.108), channel_id=4, replica_groups=mesh['section'=2,'dp'=8,'tensor'=2] {'dp'}, dimensions={2}, use_global_device_ids=true | all-gather | bytes 3456 | tf_op jit(solution)/shard_map/all_gather | solution.py:224
  103.2 32.1 %all-gather.3 = bf16[1,2,768]{1,0,2:T(2,128)(2,1)S(1)} all-gather(bf16[1,2,96]{1,0,2:T(2,128)(2,1)S(1)} %copy.109), channel_id=5, replica_groups=mesh['section'=2,'dp'=8,'tensor'=2] {'dp'}, dimensions={2}, use_global_device_ids=true | all-gather | bytes 3456 | tf_op jit(solution)/shard_map/all_gather | solution.py:225
  135.3 4.6 fusion.211
  139.9 4.6 fusion.210
  148.0 11.8 all-gather.12.cloned.1.call-done
  159.9 11.7 fusion.8
  171.6 41.2 %all-gather.14.cloned.1.call-done = bf16[1,1536,768]{1,2,0:T(8,128)(2,1)} async-done(((bf16[1,1536,96]{1,2,0:T(8,128)(2,1)}), bf16[1,1536,768]{1,2,0:T(8,128)(2,1)}) %all-gather.14.cloned.1.call-update) | async-done | bytes 2359312 | tf_op jit(solution)/shard_map/all_gather | solution.py:223
  212.8 4.4 fusion.159
  217.3 33.0 %all-reduce.15.cloned.1.call-done = bf16[512,768]{1,0:T(8,128)(2,1)} async-done(((bf16[512,768]{1,0:T(8,128)(2,1)}), bf16[512,768]{1,0:T(8,128)(2,1)}) %all-reduce.15.cloned.1.call-update) | async-done | bytes 786448 | tf_op jit(solution)/shard_map/psum | solution.py:51
  265.9 34.5 %all-reduce.17.cloned.1.call-done = bf16[512,768]{1,0:T(8,128)(2,1)} async-done(((bf16[512,768]{1,0:T(8,128)(2,1)}), bf16[512,768]{1,0:T(8,128)(2,1)}) %all-reduce.17.cloned.1.call-update) | async-done | bytes 786448 | tf_op jit(solution)/shard_map/psum | solution.py:51
  302.5 9.4 fusion.11
  315.4 34.4 %all-reduce.19.cloned.1.call-done = bf16[512,768]{1,0:T(8,128)(2,1)} async-done(((bf16[512,768]{1,0:T(8,128)(2,1)}), bf16[512,768]{1,0:T(8,128)(2,1)}) %all-reduce.19.cloned.1.call-update) | async-done | bytes 786448 | tf_op jit(solution)/shard_map/psum | solution.py:51
  364.3 34.5 %all-reduce.21.cloned.1.call-done = bf16[512,768]{1,0:T(8,128)(2,1)} async-done(((bf16[512,768]{1,0:T(8,128)(2,1)}), bf16[512,768]{1,0:T(8,128)(2,1)}) %all-reduce.21.cloned.1.call-update) | async-done | bytes 786448 | tf_op jit(solution)/shard_map/psum | solution.py:51
  401.1 11.1 fusion.14
  415.8 34.4 %all-reduce.23.cloned.1.call-done = bf16[512,768]{1,0:T(8,128)(2,1)} async-done(((bf16[512,768]{1,0:T(8,128)(2,1)}), bf16[512,768]{1,0:T(8,128)(2,1)}) %all-reduce.23.cloned.1.call-update) | async-done | bytes 786448 | tf_op jit(solution)/shard_map/psum | solution.py:51
  463.2 34.0 %all-reduce.25.cloned.1.call-done = bf16[512,768]{1,0:T(8,128)(2,1)} async-done(((bf16[512,768]{1,0:T(8,128)(2,1)}), bf16[512,768]{1,0:T(8,128)(2,1)}) %all-reduce.25.cloned.1.call-update) | async-done | bytes 786448 | tf_op jit(solution)/shard_map/psum | solution.py:55
  524.5 34.4 %all-reduce.27.cloned.1.call-done = bf16[512,768]{1,0:T(8,128)(2,1)} async-done(((bf16[512,768]{1,0:T(8,128)(2,1)}), bf16[512,768]{1,0:T(8,128)(2,1)}) %all-reduce.27.cloned.1.call-update) | async-done | bytes 786448 | tf_op jit(solution)/shard_map/psum | solution.py:55
  576.0 34.4 %all-reduce.29.cloned.1.call-done = bf16[512,768]{1,0:T(8,128)(2,1)} async-done(((bf16[512,768]{1,0:T(8,128)(2,1)}), bf16[512,768]{1,0:T(8,128)(2,1)}) %all-reduce.29.cloned.1.call-update) | async-done | bytes 786448 | tf_op jit(solution)/shard_map/psum | solution.py:55
  631.2 34.4 %all-reduce.31.cloned.1.call-done = bf16[512,768]{1,0:T(8,128)(2,1)} async-done(((bf16[512,768]{1,0:T(8,128)(2,1)}), bf16[512,768]{1,0:T(8,128)(2,1)}) %all-reduce.31.cloned.1.call-update) | async-done | bytes 786448 | tf_op jit(solution)/shard_map/psum | solution.py:55
  688.0 28.4 %all-reduce.33.cloned.1.call-done = bf16[512,768]{1,0:T(8,128)(2,1)} async-done(((bf16[512,768]{1,0:T(8,128)(2,1)}), bf16[512,768]{1,0:T(8,128)(2,1)}) %all-reduce.33.cloned.1.call-update) | async-done | bytes 786448 | tf_op jit(solution)/shard_map/psum | solution.py:55
  721.4 4.5 multiply_reduce_fusion
  762.8 4.2 select_add_fusion
  773.3 4.4 select_add_fusion.1
  782.3 14.8 %reduce-scatter.21.cloned.1.call-done = f32[96,2]{1,0:T(8,128)} async-done(((f32[768,2]{1,0:T(8,128)}), f32[96,2]{1,0:T(8,128)}) %reduce-scatter.21.cloned.1.call-update) | async-done | bytes 784
  798.5 62.5 %reduce-scatter.19.cloned.1.call-done = f32[96,2]{1,0:T(8,128)} async-done(((f32[768,2]{1,0:T(8,128)}), f32[96,2]{1,0:T(8,128)}) %reduce-scatter.19.cloned.1.call-update) | async-done | bytes 784
  862.4 34.2 %all-reduce.35.cloned.1.call-done = bf16[512,768]{1,0:T(8,128)(2,1)} async-done(((bf16[512,768]{1,0:T(8,128)(2,1)}), bf16[512,768]{1,0:T(8,128)(2,1)}) %all-reduce.35.cloned.1.call-update) | async-done | bytes 786448 | tf_op jit(solution)/shard_map/psum | solution.py:55
  899.9 64.5 %reduce-scatter.13.cloned.1.call-done = f32[384,96]{0,1:T(8,128)} async-done(((f32[384,768]{0,1:T(8,128)}), f32[384,96]{0,1:T(8,128)}) %reduce-scatter.13.cloned.1.call-update) | async-done | bytes 147472 | tf_op jit(solution)/shard_map/reduce_scatter | solution.py:270
  964.4 82.1 %reduce-scatter.11.cloned.1.call-done = f32[96,3,384]{2,0,1:T(8,128)} async-done(((f32[768,3,384]{2,0,1:T(8,128)}), f32[96,3,384]{2,0,1:T(8,128)}) %reduce-scatter.11.cloned.1.call-update) | async-done | bytes 442384 | tf_op jit(solution)/shard_map/reduce_scatter | solution.py:269
  1046.5 98.9 %reduce-scatter.17.cloned.1.call-done = f32[1536,96]{0,1:T(8,128)} async-done(((f32[1536,768]{0,1:T(8,128)}), f32[1536,96]{0,1:T(8,128)}) %reduce-scatter.17.cloned.1.call-update) | async-done | bytes 589840 | tf_op jit(solution)/shard_map/reduce_scatter | solution.py:272
  1145.4 99.3 %reduce-scatter.15.cloned.1.call-done = f32[96,1536]{1,0:T(8,128)} async-done(((f32[768,1536]{1,0:T(8,128)}), f32[96,1536]{1,0:T(8,128)}) %reduce-scatter.15.cloned.1.call-update) | async-done | bytes 589840 | tf_op jit(solution)/shard_map/reduce_scatter | solution.py:271
  (468 shorter events, 217.7 us)
Async XLA Ops:
  7.2 53.2 %all-gather.10.cloned.1.call-start = ((), (), s32[]{:S(2)}) async-start(), calls=%async_computation.22 | async-start | bytes 1990656 | tf_op jit(solution)/shard_map/all_gather | solution.py:220
  7.9 136.7 %all-reduce.13.cloned.1.call-start = ((), (), s32[]{:S(2)}) async-start(), calls=%async_computation.6 | async-start | bytes 1572864 | tf_op jit(solution)/shard_map/psum | solution.py:51
  70.6 89.3 %all-gather.12.cloned.1.call-start = ((), (), s32[]{:S(2)}) async-start(), calls=%async_computation.23 | async-start | bytes 2654208 | tf_op jit(solution)/shard_map/all_gather | solution.py:222
  71.3 141.5 %all-gather.14.cloned.1.call-start = ((), (), s32[]{:S(2)}) async-start(), calls=%async_computation.24 | async-start | bytes 2654208 | tf_op jit(solution)/shard_map/all_gather | solution.py:223
  71.9 178.4 %all-reduce.15.cloned.1.call-start = ((), (), s32[]{:S(2)}) async-start(), calls=%async_computation.7 | async-start | bytes 1572864 | tf_op jit(solution)/shard_map/psum | solution.py:51
  146.4 103.8 %copy-start.71 = (f32[512]{0:T(512)}, f32[512]{0:T(512)S(1)}, u32[]{:S(2)}) copy-start(f32[512]{0:T(512)S(1)} %broadcast_multiply_fusion.17) | copy-start | bytes 6148
  217.2 83.1 %all-reduce.17.cloned.1.call-start = ((), (), s32[]{:S(2)}) async-start(), calls=%async_computation.8 | async-start | bytes 1572864 | tf_op jit(solution)/shard_map/psum | solution.py:51
  253.5 3.8 collective-permute-start
  257.3 356.6 %copy-start.9 = (bf16[1,512,768]{2,1,0:T(8,128)(2,1)}, bf16[1,512,768]{2,1,0:T(8,128)(2,1)S(1)}, u32[]{:S(2)}) copy-start(bf16[1,512,768]{2,1,0:T(8,128)(2,1)S(1)} %dynamic-slice_select_fusion.4) | copy-start | bytes 2359300
  265.8 84.1 %all-reduce.19.cloned.1.call-start = ((), (), s32[]{:S(2)}) async-start(), calls=%async_computation.9 | async-start | bytes 1572864 | tf_op jit(solution)/shard_map/psum | solution.py:51
  315.4 83.4 %all-reduce.21.cloned.1.call-start = ((), (), s32[]{:S(2)}) async-start(), calls=%async_computation.10 | async-start | bytes 1572864 | tf_op jit(solution)/shard_map/psum | solution.py:51
  351.9 216.1 %copy-start.5 = (f32[512,768]{1,0:T(8,128)}, f32[512,768]{1,0:T(8,128)S(1)}, u32[]{:S(2)}) copy-start(f32[512,768]{1,0:T(8,128)S(1)} %get-tuple-element.222) | copy-start | bytes 4718596
  352.2 215.8 %copy-start.79 = (f32[512]{0:T(512)}, f32[512]{0:T(512)S(1)}, u32[]{:S(2)}) copy-start(f32[512]{0:T(512)S(1)} %add_rsqrt_fusion.2) | copy-start | bytes 6148
  352.6 3.9 collective-permute-start.1
  364.3 85.9 %all-reduce.23.cloned.1.call-start = ((), (), s32[]{:S(2)}) async-start(), calls=%async_computation.11 | async-start | bytes 1572864 | tf_op jit(solution)/shard_map/psum | solution.py:51
  415.7 81.5 %all-reduce.25.cloned.1.call-start = ((), (), s32[]{:S(2)}) async-start(), calls=%async_computation.12 | async-start | bytes 1572864 | tf_op jit(solution)/shard_map/psum | solution.py:55
  462.7 96.2 %all-reduce.27.cloned.1.call-start = ((), (), s32[]{:S(2)}) async-start(), calls=%async_computation.13 | async-start | bytes 1572864 | tf_op jit(solution)/shard_map/psum | solution.py:55
  524.4 86.0 %all-reduce.29.cloned.1.call-start = ((), (), s32[]{:S(2)}) async-start(), calls=%async_computation.14 | async-start | bytes 1572864 | tf_op jit(solution)/shard_map/psum | solution.py:55
  561.7 4.2 collective-permute-start.2
  575.9 89.7 %all-reduce.31.cloned.1.call-start = ((), (), s32[]{:S(2)}) async-start(), calls=%async_computation.15 | async-start | bytes 1572864 | tf_op jit(solution)/shard_map/psum | solution.py:55
  631.1 85.3 %all-reduce.33.cloned.1.call-start = ((), (), s32[]{:S(2)}) async-start(), calls=%async_computation.16 | async-start | bytes 1572864 | tf_op jit(solution)/shard_map/psum | solution.py:55
  667.9 4.5 collective-permute-start.3
  681.9 115.2 %reduce-scatter.21.cloned.1.call-start = ((), (), s32[]{:S(2)}) async-start(), calls=%async_computation.26 | async-start | bytes 442368
  735.5 125.5 %reduce-scatter.19.cloned.1.call-start = ((), (), s32[]{:S(2)}) async-start(), calls=%async_computation.25 | async-start | bytes 442368
  739.7 156.9 %all-reduce.35.cloned.1.call-start = ((), (), s32[]{:S(2)}) async-start(), calls=%async_computation.17 | async-start | bytes 1572864 | tf_op jit(solution)/shard_map/psum | solution.py:55
  744.1 220.3 %reduce-scatter.13.cloned.1.call-start = ((), (), s32[]{:S(2)}) async-start(), calls=%async_computation.19 | async-start | bytes 1327104 | tf_op jit(solution)/shard_map/reduce_scatter | solution.py:270
  749.5 297.0 %reduce-scatter.11.cloned.1.call-start = ((), (), s32[]{:S(2)}) async-start(), calls=%async_computation.18 | async-start | bytes 3981312 | tf_op jit(solution)/shard_map/reduce_scatter | solution.py:269
  757.2 388.2 %reduce-scatter.17.cloned.1.call-start = ((), (), s32[]{:S(2)}) async-start(), calls=%async_computation.21 | async-start | bytes 5308416 | tf_op jit(solution)/shard_map/reduce_scatter | solution.py:272
  767.0 477.7 %reduce-scatter.15.cloned.1.call-start = ((), (), s32[]{:S(2)}) async-start(), calls=%async_computation.20 | async-start | bytes 5308416 | tf_op jit(solution)/shard_map/reduce_scatter | solution.py:271
  780.3 116.3 %copy-start.29 = (f32[512,768]{1,0:T(8,128)S(1)}, f32[512,768]{1,0:T(8,128)}, u32[]{:S(2)}) copy-start(f32[512,768]{1,0:T(8,128)} %copy-done.27) | copy-start | bytes 4718596
  782.3 115.6 %copy-start.42 = (bf16[1,1,512,768]{3,2,1,0:T(8,128)(2,1)S(1)}, bf16[1,1,512,768]{3,2,1,0:T(8,128)(2,1)}, u32[]{:S(2)}) copy-start(bf16[1,1,512,768]{3,2,1,0:T(8,128)(2,1)} %get-tuple-element.225) | copy-start | bytes 2359300
  782.3 115.6 %copy-start.43 = (bf16[1,1,512,768]{3,2,1,0:T(8,128)(2,1)S(1)}, bf16[1,1,512,768]{3,2,1,0:T(8,128)(2,1)}, u32[]{:S(2)}) copy-start(bf16[1,1,512,768]{3,2,1,0:T(8,128)(2,1)} %get-tuple-element.227) | copy-start | bytes 2359300
  (124 other events, 1015.2 us)
Sparse Core Ops, SparseCore 0:
  10.2 50.0 all-gather.9
  70.7 33.6 all-reduce.12
  106.9 52.9 all-gather.11
  162.1 50.6 all-gather.13
  217.4 32.8 all-reduce.14
  265.9 34.3 all-reduce.16
  315.5 34.3 all-reduce.18
  364.4 34.3 all-reduce.20
  415.8 34.3 all-reduce.22
  462.8 34.3 all-reduce.24
  524.6 34.3 all-reduce.26
  576.1 34.3 all-reduce.28
  631.2 34.3 all-reduce.30
  682.1 34.3 all-reduce.32
  735.7 61.3 reduce-scatter.20
  800.6 60.3 reduce-scatter.18
  863.2 33.3 all-reduce.34
  900.4 63.9 reduce-scatter.12
  968.6 77.8 reduce-scatter.10
  1050.6 94.7 reduce-scatter.16
  1149.6 94.9 reduce-scatter.14
where the time goes:
time: 1260 us; the launch traced here: 1250 us
  waiting for transfers between devices  873 us (69%)
  matrix products  141 us (11%)
  blocking collectives  97.2 us (8%)
  other arithmetic  69.6 us (6%)
  local copies, waits for them, and re-layouts  46.7 us (4%)
  between operations  16.3 us (1%)
    psum x6, waiting for transfers between devices, back_sum(): lax.psum(partial_value.astype(jnp.bfloat16), 'tensor').astype(jnp.float32)  200 us
    psum x6, waiting for transfers between devices, tensor_sum(): lax.psum(partial_value.astype(jnp.bfloat16), 'tensor').astype(jnp.float32)  171 us
    reduce_scatter x1, waiting for transfers between devices, shards(): lax.psum_scatter(totals[2], 'dp', scatter_dimension=0, tiled=True)  99.3 us
    reduce_scatter x1, waiting for transfers between devices, shards(): lax.psum_scatter(totals[3], 'dp', scatter_dimension=1, tiled=True)  98.9 us
    reduce_scatter x1, waiting for transfers between devices, shards(): lax.psum_scatter(totals[0], 'dp', scatter_dimension=0, tiled=True)  82.1 us
    unnamed x23, waiting for transfers between devices  79.5 us
    reduce_scatter x1, waiting for transfers between devices, shards(): lax.psum_scatter(totals[1], 'dp', scatter_dimension=1, tiled=True)  64.5 us
    all_gather x1, waiting for transfers between devices, shards(): lax.all_gather(w_down[0], 'dp', axis=1, tiled=True)  41.2 us
  transfers between devices with their start and end apart: 25, of which 24 were waited for; matrix products, arithmetic and copies ran while one was open for 6% of the time, Pallas kernels for 0%

commit v1 on v0

v1 whole, which is shorter than its diff:
```python
import jax
import jax.numpy as jnp
from jax import lax
from jax.sharding import PartitionSpec as P

HEAD = 64


norm_eps = 1e-06
score_scale = 0.125
masked_value = -1000000000.0


def partner_of(segment_ids, partner):
    table = jnp.arange(partner.shape[-1], dtype=jnp.int32)
    hits = segment_ids[..., None] == table
    return jnp.sum(jnp.where(hits, partner[None, :], 0), -1)


def layer_norm(values, gain, shift):
    center = values - jnp.mean(values, -1, keepdims=True)
    inverse = lax.rsqrt(jnp.mean(center * center, -1, keepdims=True) + norm_eps)
    normed = center * inverse
    return (normed * gain + shift, normed, inverse)


def norm_back(grad, normed, inverse, gain):
    scaled = grad * gain
    inner = (
        scaled
        - jnp.mean(scaled, -1, keepdims=True)
        - normed * jnp.mean(scaled * normed, -1, keepdims=True)
    )
    return inner * inverse


def gelu_slope(values):
    lower = 0.5 * (1.0 + lax.erf(values * 0.7071067811865476))
    density = jnp.exp(-0.5 * values * values) * 0.3989422804014327
    return lower + values * density


def swapped(value, axis):
    size = lax.axis_size(axis)
    return lax.ppermute(value, axis, [(i, size - 1 - i) for i in range(size)])


def tensor_sum(partial_value):
    low = partial_value.astype(jnp.bfloat16)
    return low.astype(jnp.float32) + swapped(low, "tensor").astype(jnp.float32)


def masked_scores(query, key, query_groups, key_groups):
    scores = (
        jnp.einsum("qhd,khd->hqk", query, key, preferred_element_type=jnp.float32) * score_scale
    )
    allowed = query_groups[:, None] == key_groups[None, :]
    return jnp.where(allowed[None], scores, masked_value)


def attend(query, key, value, query_groups, key_groups):
    scores = masked_scores(query, key, query_groups, key_groups)
    top = jnp.max(scores, -1, keepdims=True)
    expo = jnp.exp(scores - top)
    total = jnp.sum(expo, -1, keepdims=True)
    probs = (expo / total).astype(jnp.bfloat16)
    mixed = jnp.einsum("hqk,khd->qhd", probs, value, preferred_element_type=jnp.float32)
    return (mixed.astype(jnp.bfloat16), (top + jnp.log(total))[..., 0])


def attend_back(query, key, value, query_groups, key_groups, spread, grad_mixed):
    scores = masked_scores(query, key, query_groups, key_groups)
    probs = jnp.exp(scores - spread[..., None])
    probs_low = probs.astype(jnp.bfloat16)
    grad_probs = jnp.einsum("qhd,khd->hqk", grad_mixed, value, preferred_element_type=jnp.float32)
    grad_value = jnp.einsum(
        "hqk,qhd->khd", probs_low, grad_mixed, preferred_element_type=jnp.float32
    )
    row_dot = jnp.sum(probs * grad_probs, -1, keepdims=True)
    grad_scores = (probs * (grad_probs - row_dot)).astype(jnp.bfloat16)
    grad_query = (
        jnp.einsum("hqk,khd->qhd", grad_scores, key, preferred_element_type=jnp.float32)
        * score_scale
    )
    grad_key = (
        jnp.einsum("hqk,qhd->khd", grad_scores, query, preferred_element_type=jnp.float32)
        * score_scale
    )
    return jnp.stack(
        [
            grad_query.astype(jnp.bfloat16),
            grad_key.astype(jnp.bfloat16),
            grad_value.astype(jnp.bfloat16),
        ],
        1,
    )


def layer_forward(flat, weights, query_groups, key_groups):
    w_qkv, w_out, w_up, w_down, gains, shifts = weights
    length = flat.shape[0]
    local = w_qkv.shape[2]
    packed = jnp.einsum("nd,dcm->ncm", flat, w_qkv, preferred_element_type=jnp.float32).astype(
        jnp.bfloat16
    )
    heads = packed.reshape(length, 3, local // HEAD, HEAD)
    mixed, spread = attend(heads[:, 0], heads[:, 1], heads[:, 2], query_groups, key_groups)
    mixed_flat = mixed.reshape(length, local)
    attn_out = tensor_sum(jnp.dot(mixed_flat, w_out, preferred_element_type=jnp.float32))
    hidden, normed_first, inverse_first = layer_norm(
        flat.astype(jnp.float32) + attn_out, gains[0], shifts[0]
    )
    hidden_low = hidden.astype(jnp.bfloat16)
    pre = jnp.dot(hidden_low, w_up, preferred_element_type=jnp.float32)
    act = jax.nn.gelu(pre, approximate=False).astype(jnp.bfloat16)
    ffn_out = tensor_sum(jnp.dot(act, w_down, preferred_element_type=jnp.float32))
    result, normed_second, inverse_second = layer_norm(hidden + ffn_out, gains[1], shifts[1])
    kept = (
        flat,
        heads,
        spread,
        mixed_flat,
        normed_first,
        inverse_first,
        hidden_low,
        pre,
        act,
        normed_second,
        inverse_second,
    )
    return (result.astype(jnp.bfloat16), kept)


def layer_backward(grad_result, kept, weights, query_groups, key_groups):
    w_qkv, w_out, w_up, w_down, gains, shifts = weights
    (
        flat,
        heads,
        spread,
        mixed_flat,
        normed_first,
        inverse_first,
        hidden_low,
        pre,
        act,
        normed_second,
        inverse_second,
    ) = kept
    length = flat.shape[0]
    local = w_qkv.shape[2]
    gain_second = jnp.sum(grad_result * normed_second, 0)
    shift_second = jnp.sum(grad_result, 0)
    grad_sum2 = norm_back(grad_result, normed_second, inverse_second, gains[1])
    grad_ffn = grad_sum2.astype(jnp.bfloat16)
    grad_down = jnp.einsum("nf,nd->fd", act, grad_ffn, preferred_element_type=jnp.float32)
    grad_act = jnp.einsum("nd,fd->nf", grad_ffn, w_down, preferred_element_type=jnp.float32)
    grad_pre = (grad_act * gelu_slope(pre)).astype(jnp.bfloat16)
    grad_up = jnp.einsum("nd,nf->df", hidden_low, grad_pre, preferred_element_type=jnp.float32)
    grad_hidden = grad_sum2 + tensor_sum(
        jnp.einsum("nf,df->nd", grad_pre, w_up, preferred_element_type=jnp.float32)
    )
    gain_first = jnp.sum(grad_hidden * normed_first, 0)
    shift_first = jnp.sum(grad_hidden, 0)
    grad_resid = norm_back(grad_hidden, normed_first, inverse_first, gains[0])
    grad_attn = grad_resid.astype(jnp.bfloat16)
    grad_out = jnp.einsum("nm,nd->md", mixed_flat, grad_attn, preferred_element_type=jnp.float32)
    grad_mixed = jnp.einsum(
        "nd,md->nm", grad_attn, w_out, preferred_element_type=jnp.float32
    ).astype(jnp.bfloat16)
    grad_mixed = grad_mixed.reshape(length, local // HEAD, HEAD)
    grad_heads = attend_back(
        heads[:, 0], heads[:, 1], heads[:, 2], query_groups, key_groups, spread, grad_mixed
    )
    grad_packed = grad_heads.reshape(length, 3, local)
    grad_qkv = jnp.einsum("nd,ncm->dcm", flat, grad_packed, preferred_element_type=jnp.float32)
    grad_input = grad_resid + tensor_sum(
        jnp.einsum("ncm,dcm->nd", grad_packed, w_qkv, preferred_element_type=jnp.float32)
    )
    grads = (
        grad_qkv.astype(jnp.bfloat16),
        grad_out.astype(jnp.bfloat16),
        grad_up.astype(jnp.bfloat16),
        grad_down.astype(jnp.bfloat16),
        jnp.stack([gain_first, gain_second]),
        jnp.stack([shift_first, shift_second]),
    )
    return (grads, grad_input.astype(jnp.bfloat16))


def shards(
    inputs, segments, partner, grad_output, w_qkv, w_out, w_up, w_down, norm_gain, norm_shift
):
    core = lax.axis_index("section")
    rows = inputs.shape[0] // lax.axis_size("section")

    def per_row(row):
        key_groups = lax.dynamic_index_in_dim(segments, row, 0, False)
        mapped = partner_of(key_groups, lax.dynamic_index_in_dim(partner, row, 0, False))
        flat = lax.dynamic_index_in_dim(inputs, row, 0, False)
        first, kept_first = layer_forward(flat, layers[0], key_groups, key_groups)
        second, kept_second = layer_forward(first, layers[1], mapped, key_groups)
        grad_top = lax.dynamic_index_in_dim(grad_output, row, 0, False).astype(jnp.float32)
        grads_second, grad_mid = layer_backward(
            grad_top, kept_second, layers[1], mapped, key_groups
        )
        grads_first, grad_low = layer_backward(
            grad_mid.astype(jnp.float32), kept_first, layers[0], key_groups, key_groups
        )
        return (first, second, grad_low, grad_mid, grads_first, grads_second)

    def gathered(shard, axis):
        own = lax.all_gather(shard[0], "dp", axis=axis, tiled=True)
        other = swapped(own, "section")
        return (jnp.where(core == 0, own, other), jnp.where(core == 0, other, own))

    pairs = [
        gathered(w_qkv, 0),
        gathered(w_out, 1),
        gathered(w_up, 0),
        gathered(w_down, 1),
        gathered(norm_gain, 1),
        gathered(norm_shift, 1),
    ]
    layers = [
        [pair[layer].astype(jnp.float32) if place > 3 else pair[layer] for place, pair in enumerate(pairs)]
        for layer in range(2)
    ]
    done = [per_row(core * rows + step) for step in range(rows)]

    def summed(first, second, axis):
        mine = jnp.where(core == 0, first, second)
        away = jnp.where(core == 0, second, first)
        both = mine.astype(jnp.float32) + swapped(away, "section").astype(jnp.float32)
        return lax.psum_scatter(both.astype(first.dtype), "dp", scatter_dimension=axis, tiled=True).astype(jnp.float32)

    def total(layer, place):
        value = done[0][4 + layer][place]
        for item in done[1:]:
            value = (value.astype(jnp.float32) + item[4 + layer][place].astype(jnp.float32)).astype(value.dtype)
        return value

    axes = (0, 1, 0, 1, 1, 1)
    sums = [summed(total(0, place), total(1, place), axis) for place, axis in enumerate(axes)]

    def regrouped(first, second):
        mine = jnp.where(core == 0, first, second)
        other = swapped(jnp.where(core == 0, second, first), "section")
        return jnp.where(
            core == 0, jnp.concatenate([mine, other]), jnp.concatenate([other, mine])
        )

    layer_outputs = regrouped(
        jnp.stack([item[0] for item in done]), jnp.stack([item[1] for item in done])
    )
    input_grads = regrouped(
        jnp.stack([item[2] for item in done]), jnp.stack([item[3] for item in done])
    )
    return (layer_outputs[None], input_grads[None]) + tuple(value[None] for value in sums)


def solution(mesh):
    placed = (
        P("dp", None, None),
        P("dp", None),
        P("dp", None),
        P("dp", None, None),
        P("section", "dp", None, "tensor"),
        P("section", "tensor", "dp"),
        P("section", "dp", "tensor"),
        P("section", "tensor", "dp"),
        P("section", None, "dp"),
        P("section", None, "dp"),
    )
    return jax.shard_map(
        shards,
        mesh=mesh,
        in_specs=placed,
        out_specs=(
            P("section", "dp", None, None),
            P("section", "dp", None, None),
            P("section", "dp", None, "tensor"),
            P("section", "tensor", "dp"),
            P("section", "dp", "tensor"),
            P("section", "tensor", "dp"),
            P("section", None, "dp"),
            P("section", None, "dp"),
        ),
        check_vma=False,
    )
```

time: 1260 us -> 819 us (0.65)
  waiting for transfers between devices: 873 us -> 506 us
  matrix products: 141 us -> 102 us
  other arithmetic: 69.6 us -> 38.9 us
    psum x12 -> x0, waiting for transfers between devices: 371 us -> none  [the longest x6 200 us: back_sum(): lax.psum(partial_value.astype(jnp.bfloat16), 'tensor').astype(jnp.float32)]
    reduce_scatter x4 -> x2, waiting for transfers between devices: 345 us -> 136 us  [summed(): lax.psum_scatter(both.astype(first.dtype), 'dp', scatter_dimension=axis,...]
    ppermute x4 -> x22, waiting for transfers between devices: 8.83 us -> 114 us  [swapped(): return lax.ppermute(value, axis, [(i, size - 1 - i) for i in range(size)])]
    unnamed x23 -> x13, waiting for transfers between devices: 79.5 us -> 184 us
    dot_general x3 -> x2, matrix products: 32.2 us -> 19.6 us  [layer_forward(): pre = jnp.dot(hidden_low, w_up, preferred_element_type=jnp.float32)]
    unnamed x268 -> x226, local copies, waits for them, and re-layouts: 29.7 us -> 23.6 us
  transfers between devices with their start and end apart: 25 -> 31, of which waited for: 24 -> 18; matrix products, arithmetic and copies ran while one was open for 6% -> 10% of each run, Pallas kernels for 0% -> 0%
where the time goes in v1:
time: 819 us; the launch traced here: 812 us
  waiting for transfers between devices  506 us (62%)
  matrix products  102 us (12%)
  blocking collectives  96 us (12%)
  local copies, waits for them, and re-layouts  42.7 us (5%)
  other arithmetic  38.9 us (5%)
  between operations  15.5 us (2%)
  starting transfers between devices  10.9 us (1%)
    unnamed x13, waiting for transfers between devices  184 us
    reduce_scatter x2, waiting for transfers between devices, summed(): lax.psum_scatter(both.astype(first.dtype), 'dp', scatter_dimension=axis,...  136 us
    ppermute x22, waiting for transfers between devices, swapped(): return lax.ppermute(value, axis, [(i, size - 1 - i) for i in range(size)])  114 us
    all_gather x3, blocking collectives, gathered(): own = lax.all_gather(shard[0], 'dp', axis=axis, tiled=True)  96 us
    all_gather x3, waiting for transfers between devices, gathered(): own = lax.all_gather(shard[0], 'dp', axis=axis, tiled=True)  71.9 us
    unnamed x226, local copies, waits for them, and re-layouts  23.6 us
    dot_general x2, matrix products, layer_forward(): pre = jnp.dot(hidden_low, w_up, preferred_element_type=jnp.float32)  19.6 us
  transfers between devices with their start and end apart: 31, of which 18 were waited for; matrix products, arithmetic and copies ran while one was open for 10% of the time, Pallas kernels for 0%

profile of v1, /device:TPU:0, one launch (start us, length us, event | category | flops | bytes accessed | tf_op | source)
XLA Modules:
  0.0 811.9 jit_solution(18100717246168206088)
XLA Ops:
  8.7 49.9 %all-gather.10.cloned.1.call-done = bf16[1,768,3,384]{3,1,2,0:T(8,128)(2,1)} async-done(((bf16[1,96,3,384]{3,1,2,0:T(8,128)(2,1)}), bf16[1,768,3,384]{3,1,2,0:T(8,128)(2,1)}) %all-gather.10.cloned.1.call-update) | async-done | bytes 1769488 | tf_op jit(solution)/shard_map/all_gather | solution.py:212
  58.7 32.3 %all-gather.1 = bf16[1,384,768]{1,2,0:T(8,128)(2,1)S(1)} all-gather(bf16[1,384,96]{1,2,0:T(8,128)(2,1)} %param.15), channel_id=3, replica_groups=mesh['section'=2,'dp'=8,'tensor'=2] {'dp'}, dimensions={2}, use_global_device_ids=true | all-gather | bytes 663552 | tf_op jit(solution)/shard_map/all_gather | solution.py:212
  91.8 22.0 %all-gather.12.cloned.1.call-done = bf16[1,768,1536]{2,1,0:T(8,128)(2,1)} async-done(((bf16[1,96,1536]{2,1,0:T(8,128)(2,1)}), bf16[1,768,1536]{2,1,0:T(8,128)(2,1)}) %all-gather.12.cloned.1.call-update) | async-done | bytes 2359312 | tf_op jit(solution)/shard_map/all_gather | solution.py:212
  124.1 32.1 %all-gather.2 = bf16[1,2,768]{1,0,2:T(2,128)(2,1)S(1)} all-gather(bf16[1,2,96]{1,0,2:T(2,128)(2,1)S(1)} %copy.95), channel_id=4, replica_groups=mesh['section'=2,'dp'=8,'tensor'=2] {'dp'}, dimensions={2}, use_global_device_ids=true | all-gather | bytes 3456 | tf_op jit(solution)/shard_map/all_gather | solution.py:212
  156.7 31.7 %all-gather.3 = bf16[1,2,768]{1,0,2:T(2,128)(2,1)S(1)} all-gather(bf16[1,2,96]{1,0,2:T(2,128)(2,1)S(1)} %copy.97), channel_id=5, replica_groups=mesh['section'=2,'dp'=8,'tensor'=2] {'dp'}, dimensions={2}, use_global_device_ids=true | all-gather | bytes 3456 | tf_op jit(solution)/shard_map/all_gather | solution.py:212
  190.0 4.4 copy.99
  197.2 9.6 %fusion.6 = (bf16[512,1536]{1,0:T(8,128)(2,1)S(1)}, f32[512,1536]{1,0:T(8,128)}) fusion(bf16[768,1536]{1,0:T(8,128)(2,1)} %collective-permute-done.5, pred[]{:T(512)S(6)} %eq.28, bf16[1,768,1536]{2,1,0:T(8,128)(2,1)S(1)} %copy-done.93, f32[512,768]{1,0:T(8,128)S(1)} %get-tuple-element.75, f32[768]{0:T(1024)S(1)} %get-tuple-element.62, ...), kind=kOutput, calls=%fused_computation.31 | convolution fusion | flops 1262223360 | bytes 11020289 | tf_op jit(solution)/shard_map/dot_general | solution.py:114
  206.7 4.5 convolution_convert_fusion.11
  212.1 18.4 %collective-permute-done.7 = bf16[512,768]{1,0:T(8,128)(2,1)S(1)} collective-permute-done((bf16[512,768]{1,0:T(8,128)(2,1)S(1)}, bf16[512,768]{1,0:T(8,128)(2,1)S(1)}, u32[]{:S(2)}, u32[]{:S(2)}) %collective-permute-start.7) | collective-permute-done | bytes 786464 | tf_op jit(solution)/shard_map/ppermute | solution.py:45
  239.9 17.8 %collective-permute-done.8 = bf16[512,768]{1,0:T(8,128)(2,1)S(1)} collective-permute-done((bf16[512,768]{1,0:T(8,128)(2,1)S(1)}, bf16[512,768]{1,0:T(8,128)(2,1)S(1)}, u32[]{:S(2)}, u32[]{:S(2)}) %collective-permute-start.8) | collective-permute-done | bytes 786464 | tf_op jit(solution)/shard_map/ppermute | solution.py:45
  258.7 10.0 %fusion.9 = (bf16[512,1536]{1,0:T(8,128)(2,1)S(1)}, f32[512,1536]{1,0:T(8,128)S(1)}) fusion(bf16[768,1536]{1,0:T(8,128)(2,1)} %collective-permute-done.5, pred[]{:T(512)S(6)} %eq.28, bf16[1,768,1536]{2,1,0:T(8,128)(2,1)S(1)} %copy-done.93, f32[512,768]{1,0:T(8,128)S(1)} %get-tuple-element.71, f32[768]{0:T(1024)S(1)} %get-tuple-element.57, ...), kind=kOutput, calls=%fused_computation.34 | convolution fusion | flops 1262223360 | bytes 11020289 | tf_op jit(solution)/shard_map/dot_general | solution.py:114
  268.8 3.7 convolution_convert_fusion.10
  273.2 15.9 %collective-permute-done.9 = bf16[512,768]{1,0:T(8,128)(2,1)S(1)} collective-permute-done((bf16[512,768]{1,0:T(8,128)(2,1)S(1)}, bf16[512,768]{1,0:T(8,128)(2,1)S(1)}, u32[]{:S(2)}, u32[]{:S(2)}) %collective-permute-start.9) | collective-permute-done | bytes 786464 | tf_op jit(solution)/shard_map/ppermute | solution.py:45
  293.1 4.3 fusion.40
  297.4 3.7 convolution_convert_fusion.9
  301.9 12.8 %collective-permute-done.11 = bf16[512,768]{1,0:T(8,128)(2,1)S(1)} collective-permute-done((bf16[512,768]{1,0:T(8,128)(2,1)S(1)}, bf16[512,768]{1,0:T(8,128)(2,1)S(1)}, u32[]{:S(2)}, u32[]{:S(2)}) %collective-permute-start.11) | collective-permute-done | bytes 786464 | tf_op jit(solution)/shard_map/ppermute | solution.py:45
  333.9 3.7 bitcast_convert_fusion.1
  338.3 11.3 %collective-permute-done.12 = bf16[512,768]{1,0:T(8,128)(2,1)S(1)} collective-permute-done((bf16[512,768]{1,0:T(8,128)(2,1)S(1)}, bf16[512,768]{1,0:T(8,128)(2,1)S(1)}, u32[]{:S(2)}, u32[]{:S(2)}) %collective-permute-start.12) | collective-permute-done | bytes 786464 | tf_op jit(solution)/shard_map/ppermute | solution.py:45
  350.7 4.6 fusion.41
  361.3 8.7 %collective-permute-done.13 = bf16[512,768]{1,0:T(8,128)(2,1)S(1)} collective-permute-done((bf16[512,768]{1,0:T(8,128)(2,1)S(1)}, bf16[512,768]{1,0:T(8,128)(2,1)S(1)}, u32[]{:S(2)}, u32[]{:S(2)}) %collective-permute-start.13) | collective-permute-done | bytes 786464 | tf_op jit(solution)/shard_map/ppermute | solution.py:45
  409.3 4.8 convolution_convert_fusion.1
  418.2 3.9 broadcast_select_fusion
  423.1 4.2 collective-permute-done.19
  429.7 4.3 copy.134
  434.7 3.6 convolution_convert_fusion.3
  440.5 4.2 collective-permute-done.18
  453.2 18.3 %collective-permute-done.14 = bf16[512,768]{1,0:T(8,128)(2,1)S(1)} collective-permute-done((bf16[512,768]{1,0:T(8,128)(2,1)S(1)}, bf16[512,768]{1,0:T(8,128)(2,1)S(1)}, u32[]{:S(2)}, u32[]{:S(2)}) %collective-permute-start.14) | collective-permute-done | bytes 786464 | tf_op jit(solution)/shard_map/ppermute | solution.py:45
  475.8 50.8 %reduce-scatter.23.cloned.1.call-done = f32[96,2]{1,0:T(8,128)} async-done(((f32[768,2]{1,0:T(8,128)}), f32[96,2]{1,0:T(8,128)}) %reduce-scatter.23.cloned.1.call-update) | async-done | bytes 784
  529.5 62.0 %reduce-scatter.19.cloned.1.call-done = bf16[96,384]{1,0:T(8,128)(2,1)} async-done(((bf16[768,384]{1,0:T(8,128)(2,1)}), bf16[96,384]{1,0:T(8,128)(2,1)}) %reduce-scatter.19.cloned.1.call-update) | async-done | bytes 73744
  593.3 67.1 %reduce-scatter.15.cloned.1.call-done = bf16[96,3,384]{2,0,1:T(8,128)(2,1)} async-done(((bf16[768,3,384]{2,0,1:T(8,128)(2,1)}), bf16[96,3,384]{2,0,1:T(8,128)(2,1)}) %reduce-scatter.15.cloned.1.call-update) | async-done | bytes 221200 | tf_op jit(solution)/shard_map/reduce_scatter | solution.py:234
  662.2 69.6 %reduce-scatter.21.cloned.1.call-done = bf16[96,1536]{1,0:T(8,128)(2,1)} async-done(((bf16[768,1536]{1,0:T(8,128)(2,1)}), bf16[96,1536]{1,0:T(8,128)(2,1)}) %reduce-scatter.21.cloned.1.call-update) | async-done | bytes 294928
  734.2 69.1 %reduce-scatter.17.cloned.1.call-done = bf16[96,1536]{1,0:T(8,128)(2,1)} async-done(((bf16[768,1536]{1,0:T(8,128)(2,1)}), bf16[96,1536]{1,0:T(8,128)(2,1)}) %reduce-scatter.17.cloned.1.call-update) | async-done | bytes 294928 | tf_op jit(solution)/shard_map/reduce_scatter | solution.py:234
  (386 shorter events, 133.0 us)
Async XLA Ops:
  7.2 51.4 %all-gather.10.cloned.1.call-start = ((), (), s32[]{:S(2)}) async-start(), calls=%async_computation.8 | async-start | bytes 1990656 | tf_op jit(solution)/shard_map/all_gather | solution.py:212
  7.9 105.8 %all-gather.12.cloned.1.call-start = ((), (), s32[]{:S(2)}) async-start(), calls=%async_computation.9 | async-start | bytes 2654208 | tf_op jit(solution)/shard_map/all_gather | solution.py:212
  8.7 181.3 %all-gather.14.cloned.1.call-start = ((), (), s32[]{:S(2)}) async-start(), calls=%async_computation.10 | async-start | bytes 2654208 | tf_op jit(solution)/shard_map/all_gather | solution.py:212
  58.6 55.2 %collective-permute-start = (bf16[768,3,384]{2,0,1:T(8,128)(2,1)}, bf16[768,3,384]{2,0,1:T(8,128)(2,1)}, u32[]{:S(2)}, u32[]{:S(2)}) collective-permute-start(bf16[768,3,384]{2,0,1:T(8,128)(2,1)} %bitcast.294), channel_id=1, source_target_pairs={{0,16},{16,0},{1,17},{17,1},{2,18},{18,2},{3,19},{19,3},{4,20},{20... | collective-permute-start | bytes 5308424 | tf_op jit(solution)/shard_map/ppermute | solution.py:45
  58.6 415.8 %reduce-scatter.25.cloned.1.call-start = ((), (), s32[]{:S(2)}) async-start(), calls=%async_computation.14 | async-start | bytes 442368
  91.2 30.6 %collective-permute-start.1 = (bf16[384,768]{1,0:T(8,128)(2,1)S(1)}, bf16[384,768]{1,0:T(8,128)(2,1)S(1)}, u32[]{:S(2)}, u32[]{:S(2)}) collective-permute-start(bf16[384,768]{1,0:T(8,128)(2,1)S(1)} %bitcast.253), channel_id=1, source_target_pairs={{0,16},{16,0},{1,17},{17,1},{2,18},{18,2},{3,19},{19,3},{4,20},{20... | collective-permute-start | bytes 1769480 | tf_op jit(solution)/shard_map/ppermute | solution.py:45
  113.8 83.4 %collective-permute-start.5 = (bf16[768,1536]{1,0:T(8,128)(2,1)}, bf16[768,1536]{1,0:T(8,128)(2,1)}, u32[]{:S(2)}, u32[]{:S(2)}) collective-permute-start(bf16[768,1536]{1,0:T(8,128)(2,1)} %bitcast.293), channel_id=1, source_target_pairs={{0,16},{16,0},{1,17},{17,1},{2,18},{18,2},{3,19},{19,3},{4,20},{20... | collective-permute-start | bytes 7077896 | tf_op jit(solution)/shard_map/ppermute | solution.py:45
  122.5 72.2 %collective-permute-start.2 = (bf16[512,768]{1,0:T(8,128)(2,1)S(1)}, bf16[512,768]{1,0:T(8,128)(2,1)}, u32[]{:S(2)}, u32[]{:S(2)}) collective-permute-start(bf16[512,768]{1,0:T(8,128)(2,1)S(1)} %convolution_convert_fusion.13), channel_id=1, source_target_pairs={{0,1},{1,0},{2,3},{3,2},{4,5},{5,4},{6,7},{7,6},{8,9},{9,8},{10,11... | collective-permute-start | bytes 2359304 | tf_op jit(solution)/shard_map/ppermute | solution.py:45
  156.5 32.2 %collective-permute-start.3 = (bf16[2,768]{1,0:T(2,128)(2,1)S(1)}, bf16[2,768]{1,0:T(2,128)(2,1)S(1)}, u32[]{:S(2)}, u32[]{:S(2)}) collective-permute-start(bf16[2,768]{1,0:T(2,128)(2,1)S(1)} %bitcast.289), channel_id=1, source_target_pairs={{0,16},{16,0},{1,17},{17,1},{2,18},{18,2},{3,19},{19,3},{4,20},{20... | collective-permute-start | bytes 9224 | tf_op jit(solution)/shard_map/ppermute | solution.py:45
  188.6 1.2 collective-permute-start.4
  194.4 12.3 %collective-permute-start.6 = (bf16[1536,768]{1,0:T(8,128)(2,1)}, bf16[1536,768]{1,0:T(8,128)(2,1)S(1)}, u32[]{:S(2)}, u32[]{:S(2)}) collective-permute-start(bf16[1536,768]{1,0:T(8,128)(2,1)} %bitcast.14), channel_id=1, source_target_pairs={{0,16},{16,0},{1,17},{17,1},{2,18},{18,2},{3,19},{19,3},{4,20},{20... | collective-permute-start | bytes 7077896 | tf_op jit(solution)/shard_map/ppermute | solution.py:45
  206.7 86.4 %copy-start.95 = (bf16[1536,768]{1,0:T(8,128)(2,1)}, bf16[1536,768]{1,0:T(8,128)(2,1)S(1)}, u32[]{:S(2)}) copy-start(bf16[1536,768]{1,0:T(8,128)(2,1)S(1)} %collective-permute-done.6) | copy-start | bytes 7077892
  211.3 19.1 %collective-permute-start.7 = (bf16[512,768]{1,0:T(8,128)(2,1)S(1)}, bf16[512,768]{1,0:T(8,128)(2,1)S(1)}, u32[]{:S(2)}, u32[]{:S(2)}) collective-permute-start(bf16[512,768]{1,0:T(8,128)(2,1)S(1)} %convolution_convert_fusion.11), channel_id=1, source_target_pairs={{0,1},{1,0},{2,3},{3,2},{4,5},{5,4},{6,7},{7,6},{8,9},{9,8},{10,11... | collective-permute-start | bytes 2359304 | tf_op jit(solution)/shard_map/ppermute | solution.py:45
  238.5 19.2 %collective-permute-start.8 = (bf16[512,768]{1,0:T(8,128)(2,1)S(1)}, bf16[512,768]{1,0:T(8,128)(2,1)S(1)}, u32[]{:S(2)}, u32[]{:S(2)}) collective-permute-start(bf16[512,768]{1,0:T(8,128)(2,1)S(1)} %convolution_convert_fusion.12), channel_id=1, source_target_pairs={{0,1},{1,0},{2,3},{3,2},{4,5},{5,4},{6,7},{7,6},{8,9},{9,8},{10,11... | collective-permute-start | bytes 2359304 | tf_op jit(solution)/shard_map/ppermute | solution.py:45
  272.5 16.7 %collective-permute-start.9 = (bf16[512,768]{1,0:T(8,128)(2,1)S(1)}, bf16[512,768]{1,0:T(8,128)(2,1)S(1)}, u32[]{:S(2)}, u32[]{:S(2)}) collective-permute-start(bf16[512,768]{1,0:T(8,128)(2,1)S(1)} %convolution_convert_fusion.10), channel_id=1, source_target_pairs={{0,1},{1,0},{2,3},{3,2},{4,5},{5,4},{6,7},{7,6},{8,9},{9,8},{10,11... | collective-permute-start | bytes 2359304 | tf_op jit(solution)/shard_map/ppermute | solution.py:45
  301.2 13.5 %collective-permute-start.11 = (bf16[512,768]{1,0:T(8,128)(2,1)S(1)}, bf16[512,768]{1,0:T(8,128)(2,1)S(1)}, u32[]{:S(2)}, u32[]{:S(2)}) collective-permute-start(bf16[512,768]{1,0:T(8,128)(2,1)S(1)} %convolution_convert_fusion.9), channel_id=1, source_target_pairs={{0,1},{1,0},{2,3},{3,2},{4,5},{5,4},{6,7},{7,6},{8,9},{9,8},{10,11... | collective-permute-start | bytes 2359304 | tf_op jit(solution)/shard_map/ppermute | solution.py:45
  337.6 12.1 %collective-permute-start.12 = (bf16[512,768]{1,0:T(8,128)(2,1)S(1)}, bf16[512,768]{1,0:T(8,128)(2,1)S(1)}, u32[]{:S(2)}, u32[]{:S(2)}) collective-permute-start(bf16[512,768]{1,0:T(8,128)(2,1)S(1)} %bitcast_convert_fusion.1), channel_id=1, source_target_pairs={{0,1},{1,0},{2,3},{3,2},{4,5},{5,4},{6,7},{7,6},{8,9},{9,8},{10,11... | collective-permute-start | bytes 2359304 | tf_op jit(solution)/shard_map/ppermute | solution.py:45
  356.8 13.2 %collective-permute-start.13 = (bf16[512,768]{1,0:T(8,128)(2,1)S(1)}, bf16[512,768]{1,0:T(8,128)(2,1)S(1)}, u32[]{:S(2)}, u32[]{:S(2)}) collective-permute-start(bf16[512,768]{1,0:T(8,128)(2,1)S(1)} %convolution_convert_fusion.8), channel_id=1, source_target_pairs={{0,1},{1,0},{2,3},{3,2},{4,5},{5,4},{6,7},{7,6},{8,9},{9,8},{10,11... | collective-permute-start | bytes 2359304 | tf_op jit(solution)/shard_map/ppermute | solution.py:45
  398.7 15.4 %collective-permute-start.16 = (bf16[768,3,384]{2,0,1:T(8,128)(2,1)}, bf16[768,3,384]{2,0,1:T(8,128)(2,1)}, u32[]{:S(2)}, u32[]{:S(2)}) collective-permute-start(bf16[768,3,384]{2,0,1:T(8,128)(2,1)} %get-tuple-element.96), channel_id=1, source_target_pairs={{0,16},{16,0},{1,17},{17,1},{2,18},{18,2},{3,19},{19,3},{4,20},{20... | collective-permute-start | bytes 5308424 | tf_op jit(solution)/shard_map/ppermute | solution.py:45
  400.3 4.3 collective-permute-start.17
  400.8 1.7 collective-permute-start.21
  400.9 2.6 collective-permute-start.20
  403.5 123.2 %reduce-scatter.23.cloned.1.call-start = ((), (), s32[]{:S(2)}) async-start(), calls=%async_computation.13 | async-start | bytes 442368
  404.5 187.0 %reduce-scatter.19.cloned.1.call-start = ((), (), s32[]{:S(2)}) async-start(), calls=%async_computation.11 | async-start | bytes 663552
  409.0 251.4 %reduce-scatter.15.cloned.1.call-start = ((), (), s32[]{:S(2)}) async-start(), calls=%async_computation.6 | async-start | bytes 1990656 | tf_op jit(solution)/shard_map/reduce_scatter | solution.py:234
  417.5 314.3 %reduce-scatter.21.cloned.1.call-start = ((), (), s32[]{:S(2)}) async-start(), calls=%async_computation.12 | async-start | bytes 2654208
  422.1 5.1 collective-permute-start.19
  434.1 369.2 %reduce-scatter.17.cloned.1.call-start = ((), (), s32[]{:S(2)}) async-start(), calls=%async_computation.7 | async-start | bytes 2654208 | tf_op jit(solution)/shard_map/reduce_scatter | solution.py:234
  440.1 4.6 collective-permute-start.18
  451.1 20.4 %collective-permute-start.14 = (bf16[512,768]{1,0:T(8,128)(2,1)S(1)}, bf16[512,768]{1,0:T(8,128)(2,1)S(1)}, u32[]{:S(2)}, u32[]{:S(2)}) collective-permute-start(bf16[512,768]{1,0:T(8,128)(2,1)S(1)} %bitcast_convert_fusion), channel_id=1, source_target_pairs={{0,1},{1,0},{2,3},{3,2},{4,5},{5,4},{6,7},{7,6},{8,9},{9,8},{10,11... | collective-permute-start | bytes 2359304 | tf_op jit(solution)/shard_map/ppermute | solution.py:45
  452.6 20.5 %collective-permute-start.10 = (bf16[1,512,768]{2,1,0:T(8,128)(2,1)S(1)}, bf16[1,512,768]{2,1,0:T(8,128)(2,1)S(1)}, u32[]{:S(2)}, u32[]{:S(2)}) collective-permute-start(bf16[1,512,768]{2,1,0:T(8,128)(2,1)S(1)} %get-tuple-element.77), channel_id=1, source_target_pairs={{0,16},{16,0},{1,17},{17,1},{2,18},{18,2},{3,19},{19,3},{4,20},{20... | collective-permute-start | bytes 2359304 | tf_op jit(solution)/shard_map/ppermute | solution.py:45
  473.0 55.1 %collective-permute-start.15 = (bf16[1,512,768]{2,1,0:T(8,128)(2,1)}, bf16[1,512,768]{2,1,0:T(8,128)(2,1)S(1)}, u32[]{:S(2)}, u32[]{:S(2)}) collective-permute-start(bf16[1,512,768]{2,1,0:T(8,128)(2,1)} %select_bitcast_fusion), channel_id=1, source_target_pairs={{0,16},{16,0},{1,17},{17,1},{2,18},{18,2},{3,19},{19,3},{4,20},{20... | collective-permute-start | bytes 2359304 | tf_op jit(solution)/shard_map/ppermute | solution.py:45
  (106 other events, 1605.5 us)
Sparse Core Ops, SparseCore 0:
  10.2 48.3 all-gather.9
  60.8 52.9 all-gather.11
  116.0 54.8 all-gather.13
  403.6 58.9 reduce-scatter.24
  466.2 60.3 reduce-scatter.22
  530.4 61.0 reduce-scatter.18
  595.4 65.0 reduce-scatter.14
  663.9 67.8 reduce-scatter.20
  735.3 67.9 reduce-scatter.16

commit v2 on v1

--- a/solution.py
+++ b/solution.py
@@ -1,9 +1,14 @@
+import functools
+
 import jax
 import jax.numpy as jnp
 from jax import lax
+from jax.experimental import pallas as pl
+from jax.experimental.pallas import tpu as pltpu
 from jax.sharding import PartitionSpec as P
 
 HEAD = 64
+WIDTH = 768
 
 
 norm_eps = 1e-06
@@ -258,6 +263,887 @@
     return (layer_outputs[None], input_grads[None]) + tuple(value[None] for value in sums)
 
 
+MESH = pl.DeviceIdType.MESH
+BF = jnp.bfloat16
+F32 = jnp.float32
+CHUNK = 256
+SUB = 32
+LANES = 128
+NT = (((1,), (1,)), ((), ()))
+
+
+def dot(left, right):
+    return jnp.dot(left, right, preferred_element_type=F32)
+
+
+def dot_nt(left, right):
+    return lax.dot_general(left, right, NT, preferred_element_type=F32)
+
+
+def flat_rows(value):
+    return value.reshape(-1, value.shape[-1])
+
+
+def kernel(
+    sizes,
+    x_ref,
+    go_ref,
+    keys_ref,
+    groups_ref,
+    sq,
+    so,
+    su,
+    sd,
+    sn,
+    lo_ref,
+    ig_ref,
+    oq,
+    oo,
+    ou,
+    od,
+    on,
+    wq,
+    wo,
+    wu,
+    wd,
+    wn,
+    rq,
+    ro,
+    ru,
+    rd,
+    yq,
+    yo,
+    yu,
+    yd,
+    vq,
+    vo,
+    vu,
+    vd,
+    rn,
+    yn,
+    vn,
+    ng,
+    zin,
+    packed,
+    prob,
+    mixed,
+    norm1,
+    inv1,
+    hid,
+    act,
+    slope,
+    norm2,
+    inv2,
+    gsum,
+    gtok,
+    gmix,
+    turned,
+    gtop,
+    gin,
+    work,
+    norms,
+    xs,
+    xr,
+    local_sem,
+    out_send,
+    out_recv,
+    xs_sem,
+    xr_sem,
+    az_s,
+    az_r,
+    ay_s,
+    ay_r,
+    ac_s,
+    ac_r,
+    gc_s,
+    gc_r,
+    gy_s,
+    gy_r,
+    gz_s,
+    gz_r,
+):
+    nz, ny, length, width, local, units, eps, scale = sizes
+    chunks = length // CHUNK
+    core = lax.axis_index("section")
+    place = lax.axis_index("dp")
+    side = lax.axis_index("tensor")
+    z, y = place // ny, lax.rem(place, ny)
+    other_y = 1 - y
+    to_x = {"tensor": 1 - side}
+    to_core = {"section": 1 - core}
+    to_y = {"dp": z * ny + other_y}
+
+    def turn(k):
+        return lax.rem(z + k + nz, nz)
+
+    def to_z(k):
+        return {"dp": turn(k) * ny + y}
+
+    shard = (sq, so, su, sd, sn)
+    full = (wq, wo, wu, wd, wn)
+    summed = (rq, ro, ru, rd)
+    from_y = (yq, yo, yu, yd)
+    from_z = (vq, vo, vu, vd)
+    result = (oq, oo, ou, od)
+
+    def remote(src, dst, send, recv, target):
+        return pltpu.make_async_remote_copy(
+            src_ref=src,
+            dst_ref=dst,
+            send_sem=send,
+            recv_sem=recv,
+            device_id=target,
+            device_id_type=MESH,
+        )
+
+    def each(count, body):
+        lax.fori_loop(0, count, lambda i, none: (body(i), none)[1], 0)
+
+
+    def gather_z(l, m, k):
+        return remote(
+            shard[m], full[m].at[l, z, y], az_s.at[m, k - 1], az_r.at[m, k - 1], to_z(k)
+        )
+
+    def gather_y(l, m, k, src=None):
+        ref = full[m].at[l, turn(-k), y]
+        return remote(ref if src is None else src, ref, ay_s.at[m, k], ay_r.at[m, k], to_y)
+
+    def gather_core(l, m, k, column, src=None):
+        ref = full[m].at[l, turn(-k), column]
+        slot = k if column is y else nz + k
+        return remote(
+            ref if src is None else src, ref, ac_s.at[m, slot], ac_r.at[m, slot], to_core
+        )
+
+    def gather_start(l, *mats):
+        @pl.when(core == l)
+        def _():
+            for m in mats:
+                for k in range(1, nz):
+                    gather_z(l, m, k).start()
+                gather_y(l, m, 0, shard[m]).start()
+                gather_core(l, m, 0, y, shard[m]).start()
+                full[m][l, z, y] = shard[m][...]
+
+    def gather_pass(l, *mats):
+        @pl.when(core == l)
+        def _():
+            for m in mats:
+
+                def one(k):
+                    gather_z(l, m, k).wait_recv()
+                    gather_y(l, m, k).start()
+                    gather_core(l, m, k, y).start()
+
+                lax.fori_loop(1, nz, lambda k, none: (one(k), none)[1], 0)
+
+    def gather_end(l, *mats):
+        @pl.when(core == l)
+        def _():
+            for m in mats:
+
+                def one(k):
+                    gather_y(l, m, k).wait_recv()
+                    gather_core(l, m, k, other_y).start()
+
+                each(nz, one)
+
+        @pl.when(core != l)
+        def _():
+            for m in mats:
+
+                def one(k):
+                    gather_core(l, m, k, y).wait_recv()
+                    gather_core(l, m, k, other_y).wait_recv()
+
+                each(nz, one)
+
+    def gather_drain(l, m):
+        @pl.when(core == l)
+        def _():
+            lax.fori_loop(1, nz, lambda k, none: (gather_z(l, m, k).wait_send(), none)[1], 0)
+
+            def one(k):
+                gather_y(l, m, k).wait_send()
+                gather_core(l, m, k, y).wait_send()
+                gather_core(l, m, k, other_y).wait_send()
+
+            each(nz, one)
+
+
+    def sum_core(l, m, part):
+        column = (other_y, y)[part]
+        return remote(
+            full[m].at[l, :, column],
+            summed[m].at[:, column],
+            gc_s.at[m, part],
+            gc_r.at[m, part],
+            to_core,
+        )
+
+    def sum_y(l, m, k):
+        return remote(
+            full[m].at[l, k, other_y], from_y[m].at[k], gy_s.at[m, k], gy_r.at[m, k], to_y
+        )
+
+    def sum_z(l, m, k):
+        return remote(
+            full[m].at[l, turn(k), y],
+            from_z[m].at[k - 1],
+            gz_s.at[m, k - 1],
+            gz_r.at[m, k - 1],
+            to_z(k),
+        )
+
+    def sum_start(l, m):
+        @pl.when(core != l)
+        def _():
+            sum_core(l, m, 0).start()
+            sum_core(l, m, 1).start()
+
+    def sum_first(l, m):
+        @pl.when(core == l)
+        def _():
+            sum_core(l, m, 0).wait_recv()
+
+            def one(k):
+                both = full[m][l, k, other_y].astype(F32) + summed[m][k, other_y].astype(F32)
+                full[m][l, k, other_y] = both.astype(BF)
+                sum_y(l, m, k).start()
+
+            each(nz, one)
+
+    def sum_second(l, m):
+        @pl.when(core == l)
+        def _():
+            sum_core(l, m, 1).wait_recv()
+
+            def total(k):
+                at = turn(k)
+                sum_y(l, m, at).wait_recv()
+                both = full[m][l, at, y].astype(F32) + summed[m][at, y].astype(F32)
+                return both + from_y[m][at].astype(F32)
+
+            def one(k, none):
+                full[m][l, turn(k), y] = total(k).astype(BF)
+                sum_z(l, m, k).start()
+                return none
+
+            lax.fori_loop(1, nz, one, 0)
+            result[m][...] = total(0)
+
+    def sum_last(l, m):
+        @pl.when(core == l)
+        def _():
+            def one(k, none):
+                sum_z(l, m, k).wait_recv()
+                result[m][...] += from_z[m][k - 1].astype(F32)
+                return none
+
+            lax.fori_loop(1, nz, one, 0)
+
+    def sum_drain(l, m):
+        @pl.when(core != l)
+        def _():
+            sum_core(l, m, 0).wait_send()
+            sum_core(l, m, 1).wait_send()
+
+        @pl.when(core == l)
+        def _():
+            each(nz, lambda k: sum_y(l, m, k).wait_send())
+            lax.fori_loop(1, nz, lambda k, none: (sum_z(l, m, k).wait_send(), none)[1], 0)
+
+
+    def vec_core(l):
+        return remote(ng.at[l], rn, gc_s.at[4, 0], gc_r.at[4, 0], to_core)
+
+    def vec_y(l):
+        return remote(ng.at[2], yn, gy_s.at[4, 0], gy_r.at[4, 0], to_y)
+
+    def vec_z(l, k):
+        return remote(
+            ng.at[3], vn.at[k - 1], gz_s.at[4, k - 1], gz_r.at[4, k - 1], to_z(k)
+        )
+
+    def vec_start(l):
+        @pl.when(core != l)
+        def _():
+            vec_core(l).start()
+
+    def vec_first(l):
+        @pl.when(core == l)
+        def _():
+            vec_core(l).wait_recv()
+            ng[2] = ng[l] + rn[...]
+            vec_y(l).start()
+
+    def vec_second(l):
+        @pl.when(core == l)
+        def _():
+            vec_y(l).wait_recv()
+            ng[3] = ng[2] + yn[...]
+            for k in range(1, nz):
+                vec_z(l, k).start()
+
+    def vec_last(l):
+        @pl.when(core == l)
+        def _():
+            total = ng[3]
+            for k in range(1, nz):
+                vec_z(l, k).wait_recv()
+                total = total + vn[k - 1]
+            on[...] = total
+
+    def vec_drain(l):
+        @pl.when(core != l)
+        def _():
+            vec_core(l).wait_send()
+
+        @pl.when(core == l)
+        def _():
+            vec_y(l).wait_send()
+            for k in range(1, nz):
+                vec_z(l, k).wait_send()
+
+
+    def exchange(i, c):
+        return remote(xs.at[c], xr.at[i % 2, c], xs_sem.at[c], xr_sem.at[i % 2, c], to_x)
+
+    def send(i, c):
+        exchange(i, c).start()
+
+    def arrive(i, c):
+        exchange(i, c).wait()
+
+    def both(i, c, r):
+        rows = pl.ds(r * SUB, SUB)
+        return xs[c, rows].astype(F32) + xr[i % 2, c, rows].astype(F32)
+
+    def chunk_rows(c):
+        return pl.ds(pl.multiple_of(c * CHUNK, CHUNK), CHUNK)
+
+    def sub_rows(c, r):
+        return pl.ds(pl.multiple_of(c * CHUNK + r * SUB, SUB), SUB)
+
+    def columns(j, span):
+        return pl.ds(pl.multiple_of(j * span, LANES), span)
+
+
+    def out_copy(l, which, src, dst):
+        def away():
+            return remote(src, dst.at[core], out_send.at[which], out_recv.at[which], to_core)
+
+        def here():
+            return pltpu.make_async_copy(src, dst.at[core], local_sem.at[which])
+
+        return here, away
+
+    def out_start(l, which, src, dst):
+        here, away = out_copy(l, which, src, dst)
+
+        @pl.when(core == l)
+        def _():
+            here().start()
+
+        @pl.when(core != l)
+        def _():
+            away().start()
+
+    def out_wait(l, which, src, dst):
+        here, away = out_copy(l, which, src, dst)
+
+        @pl.when(core == l)
+        def _():
+            here().wait()
+            remote(
+                src, dst.at[1 - core], out_send.at[which], out_recv.at[which], to_core
+            ).wait_recv()
+
+        @pl.when(core != l)
+        def _():
+            away().wait_send()
+
+
+    def project(l, c):
+        rows = chunk_rows(c)
+
+        def one(j):
+            cols = columns(j, local)
+            packed[l, rows, cols] = dot(
+                zin[l, rows], flat_rows(wq[l, :, :, :, cols])
+            ).astype(BF)
+
+        each(3, one)
+
+    low_lane = lax.broadcasted_iota(jnp.int32, (1, LANES), 1) < LANES // 2
+
+    def half(value, h):
+        keep = low_lane if h == 0 else jnp.logical_not(low_lane)
+        return jnp.where(keep, value, jnp.zeros_like(value))
+
+    def attend(l, c):
+        rows = chunk_rows(c)
+        lanes = columns(c, CHUNK)
+        allowed = keys_ref[...] == groups_ref[pl.ds(l, 1), lanes]
+
+        def one(j):
+            query = packed[l, rows, columns(j, LANES)]
+            key = packed[l, :, pl.ds(pl.multiple_of(local + j * LANES, LANES), LANES)]
+            value = packed[l, :, pl.ds(pl.multiple_of(2 * local + j * LANES, LANES), LANES)]
+            value_t = value.astype(F32).T.astype(BF)
+            parts = []
+            for h in range(2):
+                scores = dot_nt(key, half(query, h)) * scale
+                scores = jnp.where(allowed, scores, -1e9)
+                top = jnp.max(scores, 0, keepdims=True)
+                expo = jnp.exp(scores - top)
+                low = (expo * (1.0 / jnp.sum(expo, 0, keepdims=True))).astype(BF)
+                prob[l, 2 * j + h, :, lanes] = low
+                parts.append(dot(value_t[h * (LANES // 2) : (h + 1) * (LANES // 2)], low))
+            mixed[l, rows, columns(j, LANES)] = jnp.concatenate(parts, 0).T.astype(BF)
+
+        each(local // LANES, one)
+
+    def send_product(i, c, left, right):
+        def one(j):
+            span = width // 2
+            xs[c, :, columns(j, span)] = dot_nt(left(), right(j)).astype(BF)
+
+        each(2, one)
+        send(i, c)
+
+    def half_rows(ref, l, j):
+        return flat_rows(ref[l, pl.ds(j * (nz // 2), nz // 2)])
+
+    def attend_out(i, l, c):
+        attend(l, c)
+        send_product(
+            i, c, lambda: mixed[l, chunk_rows(c)], lambda j: half_rows(wo, l, j)
+        )
+
+    def gather_norms(l):
+        norms[l] = jnp.sum(flat_rows(wn[l]).reshape(nz * ny, 8, width), 0)
+
+    def norm_of(l, which):
+        return norms[l, which : which + 1], norms[l, 2 + which : 3 + which]
+
+    def normalize(value):
+        center = value - jnp.mean(value, -1, keepdims=True)
+        inverse = lax.rsqrt(jnp.mean(center * center, -1, keepdims=True) + eps)
+        return center * inverse, inverse
+
+    def expand(i, l, c):
+        rows = chunk_rows(c)
+        arrive(i, c)
+        gain, shift = norm_of(l, 0)
+
+        def one(r):
+            sub = sub_rows(c, r)
+            normed, inverse = normalize(zin[l, sub].astype(F32) + both(i, c, r))
+            norm1[l, sub] = normed
+            inv1[l, sub] = inverse
+            hid[l, sub] = (normed * gain + shift).astype(BF)
+
+        each(CHUNK // SUB, one)
+
+        def tile(j):
+            span = units // 3
+            cols = columns(j, span)
+            work[...] = dot(hid[l, rows], flat_rows(wu[l, :, :, :, cols]))
+
+            def piece(r):
+                sub = sub_rows(c, r)
+                pre = work[pl.ds(pl.multiple_of(r * SUB, SUB), SUB)]
+                lower = 0.5 + 0.5 * lax.erf(pre * 0.7071067811865476)
+                density = jnp.exp(-0.5 * pre * pre) * 0.3989422804014327
+                act[l, sub, cols] = (pre * lower).astype(BF)
+                slope[l, sub, cols] = (lower + pre * density).astype(BF)
+
+            each(CHUNK // SUB, piece)
+
+        each(3, tile)
+        send_product(i + 1, c, lambda: act[l, rows], lambda j: half_rows(wd, l, j))
+
+    def second_norm(i, l, c, r):
+        sub = sub_rows(c, r)
+        gain, shift = norm_of(l, 0)
+        hidden = norm1[l, sub] * gain + shift
+        return normalize(hidden + both(i, c, r))
+
+    def norm_back(grad, normed, inverse, gain):
+        scaled = grad * gain
+        inner = (
+            scaled
+            - jnp.mean(scaled, -1, keepdims=True)
+            - normed * jnp.mean(scaled * normed, -1, keepdims=True)
+        )
+        return inner * inverse
+
+    def count(l, which, grad, normed):
+        ng[l, which : which + 1] += jnp.sum(grad * normed, 0, keepdims=True)
+        ng[l, 2 + which : 3 + which] += jnp.sum(grad, 0, keepdims=True)
+
+    def top_back(l, c, r, grad, normed, inverse):
+        sub = sub_rows(c, r)
+        count(l, 1, grad, normed)
+        back = norm_back(grad, normed, inverse, norm_of(l, 1)[0])
+        gsum[sub] = back
+        gtok[sub] = back.astype(BF)
+
+    def expand_back(i, l, c):
+        rows = chunk_rows(c)
+
+        def tile(j):
+            span = units // 3
+            cols = columns(j, span)
+            grad = dot(gtok[rows], flat_rows(wd[l, :, :, :, cols]))
+            slope[l, rows, cols] = (grad * slope[l, rows, cols].astype(F32)).astype(BF)
+
+        each(3, tile)
+        send_product(i, c, lambda: slope[l, rows], lambda j: half_rows(wu, l, j))
+
+    def weight_grad(l, m, source, right, span):
+        gather_drain(l, m)
+        step = length // 4
+
+        def flip(j):
+            rows = pl.ds(pl.multiple_of(j * step, step), step)
+            turned[:, columns(j, step)] = source[rows].astype(F32).T.astype(BF)
+
+        each(4, flip)
+
+        def tile(j):
+            cols = columns(j, span)
+            for part in range(2):
+                rows = slice(part * width // 2, (part + 1) * width // 2)
+                grad = dot(turned[rows], right(cols)).astype(BF)
+                full[m][l, part * nz // 2 : (part + 1) * nz // 2, :, :, cols] = grad.reshape(
+                    nz // 2, ny, width // (nz * ny), span
+                )
+
+        each(full[m].shape[-1] // span, tile)
+        sum_start(l, m)
+
+    def attend_back(l):
+        def one(j):
+            q_cols = columns(j, LANES)
+            k_cols = pl.ds(pl.multiple_of(local + j * LANES, LANES), LANES)
+            v_cols = pl.ds(pl.multiple_of(2 * local + j * LANES, LANES), LANES)
+            query, key, value = (packed[l, :, cols] for cols in (q_cols, k_cols, v_cols))
+            grad = gmix[:, q_cols]
+            key_t = key.astype(F32).T.astype(BF)
+            queries, keys, values = [], [], []
+            for h in range(2):
+                low = prob[l, 2 * j + h]
+                wide = low.astype(F32)
+                product = wide * dot_nt(value, half(grad, h))
+                total = jnp.sum(product, 0, keepdims=True)
+                back = (product - wide * total).astype(BF)
+                values.append(dot(low, grad))
+                keys.append(dot(back, query))
+                queries.append(dot(key_t[h * (LANES // 2) : (h + 1) * (LANES // 2)], back))
+            packed[l, :, q_cols] = (jnp.concatenate(queries, 0).T * scale).astype(BF)
+            packed[l, :, k_cols] = (jnp.where(low_lane, keys[0], keys[1]) * scale).astype(BF)
+            packed[l, :, v_cols] = jnp.where(low_lane, values[0], values[1]).astype(BF)
+
+        each(local // LANES, one)
+
+    def middle_back(i, l, c):
+        rows = chunk_rows(c)
+        arrive(i, c)
+
+        def one(r):
+            sub = sub_rows(c, r)
+            grad = gsum[sub] + both(i, c, r)
+            normed = norm1[l, sub]
+            count(l, 0, grad, normed)
+            back = norm_back(grad, normed, inv1[l, sub], norm_of(l, 0)[0])
+            gsum[sub] = back
+            gtok[sub] = back.astype(BF)
+
+        each(CHUNK // SUB, one)
+        gmix[rows] = dot(gtok[rows], flat_rows(wo[l])).astype(BF)
+
+    def project_back(i, l, c):
+        send_product(
+            i, c, lambda: packed[l, chunk_rows(c)], lambda j: half_rows(wq, l, j)
+        )
+
+
+    barrier = pltpu.get_barrier_semaphore()
+    peers = [to_x, to_core, to_y] + [to_z(k) for k in range(1, nz)]
+    for peer in peers:
+        pl.semaphore_signal(barrier, inc=1, device_id=peer, device_id_type=MESH)
+    first_rows = pltpu.make_async_copy(x_ref.at[core], zin.at[0], local_sem.at[4])
+    top_rows = pltpu.make_async_copy(go_ref.at[core], gtop, local_sem.at[5])
+    first_rows.start()
+    top_rows.start()
+    ng[...] = jnp.zeros_like(ng)
+    pl.semaphore_wait(barrier, len(peers))
+
+    Q, O, U, D, N = range(5)
+    gather_start(0, Q, N)
+    gather_start(0, O)
+    gather_pass(0, Q, N)
+    gather_start(0, U)
+    gather_end(0, Q, N)
+    first_rows.wait()
+    gather_norms(0)
+    each(chunks, lambda c: project(0, c))
+    gather_pass(0, O)
+    gather_end(0, O)
+    each(chunks, lambda c: attend_out(0, 0, c))
+    gather_pass(0, U)
+    gather_start(0, D)
+    gather_end(0, U)
+    gather_start(1, Q, N)
+    gather_pass(0, D)
+    gather_end(0, D)
+    gather_start(1, O)
+    gather_start(1, U)
+    each(chunks, lambda c: expand(0, 0, c))
+
+    gather_pass(1, Q, N)
+    gather_end(1, Q, N)
+    gather_norms(1)
+
+    def into_second(c):
+        arrive(1, c)
+        gain, shift = norm_of(0, 1)
+
+        def one(r):
+            sub = sub_rows(c, r)
+            normed, inverse = second_norm(1, 0, c, r)
+            norm2[sub] = normed
+            inv2[sub] = inverse
+            zin[1, sub] = (normed * gain + shift).astype(BF)
+
+        each(CHUNK // SUB, one)
+        project(1, c)
+
+    each(chunks, into_second)
+    out_start(0, 0, zin.at[1], lo_ref)
+    gather_pass(1, O)
+    gather_start(1, D)
+    gather_end(1, O)
+    each(chunks, lambda c: attend_out(2, 1, c))
+    gather_pass(1, U)
+    gather_end(1, U)
+    gather_pass(1, D)
+    gather_end(1, D)
+    each(chunks, lambda c: expand(2, 1, c))
+    top_rows.wait()
+
+    def over_top(c):
+        arrive(3, c)
+        gain, shift = norm_of(1, 1)
+
+        def one(r):
+            sub = sub_rows(c, r)
+            normed, inverse = second_norm(3, 1, c, r)
+            top_back(1, c, r, gtop[sub].astype(F32), normed, inverse)
+            gtop[sub] = (normed * gain + shift).astype(BF)
+
+        each(CHUNK // SUB, one)
+        expand_back(4, 1, c)
+
+    each(chunks, over_top)
+    out_start(1, 1, gtop, lo_ref)
+    third = units // 3
+    weight_grad(1, D, gtok, lambda cols: act[1, :, cols], third)
+    weight_grad(1, U, hid.at[1], lambda cols: slope[1, :, cols], third)
+    each(chunks, lambda c: middle_back(4, 1, c))
+    weight_grad(1, O, gtok, lambda cols: mixed[1, :, cols], local)
+    attend_back(1)
+    each(chunks, lambda c: project_back(5, 1, c))
+    weight_grad(1, Q, zin.at[1], lambda cols: packed[1, :, cols], local)
+    vec_start(1)
+    sum_first(1, D)
+    sum_first(1, U)
+
+    def under(c):
+        arrive(5, c)
+
+        def one(r):
+            sub = sub_rows(c, r)
+            low = (gsum[sub] + both(5, c, r)).astype(BF)
+            gin[sub] = low
+            top_back(0, c, r, low.astype(F32), norm2[sub], inv2[sub])
+
+        each(CHUNK // SUB, one)
+        expand_back(6, 0, c)
+
+    each(chunks, under)
+    out_start(1, 3, gin, ig_ref)
+    weight_grad(0, D, gtok, lambda cols: act[0, :, cols], third)
+    weight_grad(0, U, hid.at[0], lambda cols: slope[0, :, cols], third)
+    sum_second(1, D)
+    sum_second(1, U)
+    sum_first(1, O)
+    sum_first(1, Q)
+    vec_first(1)
+    each(chunks, lambda c: middle_back(6, 0, c))
+    weight_grad(0, O, gtok, lambda cols: mixed[0, :, cols], local)
+    sum_first(0, D)
+    sum_first(0, U)
+    sum_first(0, O)
+    attend_back(0)
+    each(chunks, lambda c: project_back(7, 0, c))
+    weight_grad(0, Q, zin.at[0], lambda cols: packed[0, :, cols], local)
+    vec_start(0)
+    sum_second(1, O)
+    sum_second(1, Q)
+    vec_second(1)
+    sum_last(1, D)
+    sum_last(1, U)
+    sum_second(0, D)
+    sum_first(0, Q)
+    vec_first(0)
+    sum_second(0, U)
+    sum_second(0, O)
+
+    def bottom(c):
+        arrive(7, c)
+
+        def one(r):
+            sub = sub_rows(c, r)
+            gtop[sub] = (gsum[sub] + both(7, c, r)).astype(BF)
+
+        each(CHUNK // SUB, one)
+
+    out_wait(1, 1, gtop, lo_ref)
+    each(chunks, bottom)
+    out_start(0, 2, gtop, ig_ref)
+    sum_second(0, Q)
+    vec_second(0)
+    for l in (1, 0):
+        for m in (D, U, O, Q):
+            if l == 0 or m in (O, Q):
+                sum_last(l, m)
+        vec_last(l)
+    for l in range(2):
+        for m in (Q, O, U, D):
+            sum_drain(l, m)
+        vec_drain(l)
+        gather_drain(l, N)
+    out_wait(0, 0, zin.at[1], lo_ref)
+    out_wait(0, 2, gtop, ig_ref)
+    out_wait(1, 3, gin, ig_ref)
+
+
+def fused(sizes, x, grad, keys, groups, shards_in):
+    nz, ny, length, width, local, units, eps, scale = sizes
+    block = width // (nz * ny)
+    chunks = length // CHUNK
+    spans = (3 * local, local, units, units)
+    dma = pltpu.SemaphoreType.DMA
+    vmem = pltpu.VMEM
+    scratch = [vmem((2, nz, ny, block, span), BF) for span in spans]
+    scratch += [vmem((2, nz, ny, 8, width), F32)]
+    scratch += [vmem((nz, ny, block, span), BF) for span in spans]
+    scratch += [vmem((nz, block, span), BF) for span in spans]
+    scratch += [vmem((nz - 1, block, span), BF) for span in spans]
+    scratch += [
+        vmem((8, width), F32),
+        vmem((8, width), F32),
+        vmem((nz - 1, 8, width), F32),
+        vmem((4, 8, width), F32),
+        vmem((2, length, width), BF),
+        vmem((2, length, 3 * local), BF),
+        vmem((2, local // HEAD, length, length), BF),
+        vmem((2, length, local), BF),
+        vmem((2, length, width), F32),
+        vmem((2, length, 1), F32),
+        vmem((2, length, width), BF),
+        vmem((2, length, units), BF),
+        vmem((2, length, units), BF),
+        vmem((length, width), F32),
+        vmem((length, 1), F32),
+        vmem((length, width), F32),
+        vmem((length, width), BF),
+        vmem((length, local), BF),
+        vmem((width, length), BF),
+        vmem((length, width), BF),
+        vmem((length, width), BF),
+        vmem((CHUNK, units // 3), F32),
+        vmem((2, 8, width), F32),
+        vmem((chunks, CHUNK, width), BF),
+        vmem((2, chunks, CHUNK, width), BF),
+        dma((6,)),
+        dma((4,)),
+        dma((4,)),
+        dma((chunks,)),
+        dma((2, chunks)),
+        dma((5, nz - 1)),
+        dma((5, nz - 1)),
+        dma((5, nz)),
+        dma((5, nz)),
+        dma((5, 2 * nz)),
+        dma((5, 2 * nz)),
+        dma((5, 2)),
+        dma((5, 2)),
+        dma((5, nz)),
+        dma((5, nz)),
+        dma((5, nz - 1)),
+        dma((5, nz - 1)),
+    ]
+    anywhere = pl.BlockSpec(memory_space=pl.ANY)
+    inside = pl.BlockSpec(memory_space=pltpu.VMEM)
+    return pl.pallas_call(
+        functools.partial(kernel, sizes),
+        out_shape=[jax.ShapeDtypeStruct((2, length, width), BF)] * 2
+        + [jax.ShapeDtypeStruct((block, span), F32) for span in spans]
+        + [jax.ShapeDtypeStruct((8, width), F32)],
+        in_specs=[anywhere] * 2 + [inside] * 7,
+        out_specs=[anywhere] * 2 + [inside] * 5,
+        scratch_shapes=scratch,
+        compiler_params=pltpu.CompilerParams(
+            collective_id=0, has_side_effects=True, vmem_limit_bytes=63 << 20
+        ),
+    )(x, grad, keys, groups, *shards_in)
+
+
+def kernel_shards(
+    inputs, segments, partner, grad_output, w_qkv, w_out, w_up, w_down, norm_gain, norm_shift
+):
+    core = lax.axis_index("section")
+    place = lax.axis_index("dp")
+    parts = lax.axis_size("dp")
+    length, width = inputs.shape[1:]
+    local, units = w_out.shape[1], w_up.shape[2]
+    block = width // parts
+    sizes = (parts // 2, 2, length, width, local, units, norm_eps, score_scale)
+    own = lax.dynamic_index_in_dim(segments, core, 0, False)
+    mapped = partner_of(own, lax.dynamic_index_in_dim(partner, core, 0, False))
+    keys = jnp.broadcast_to(own[:, None], (length, CHUNK))
+    groups = jnp.stack([own, mapped])
+    vectors = jnp.concatenate([norm_gain[0], norm_shift[0]]).astype(F32)
+    spread = lax.dynamic_update_slice(
+        jnp.zeros((8, width), F32), vectors, (0, place * block)
+    )
+    shards_in = (
+        w_qkv[0].reshape(block, 3 * local),
+        w_out[0].T,
+        w_up[0],
+        w_down[0].T,
+        spread,
+    )
+    outs = fused(sizes, inputs, grad_output, keys, groups, shards_in)
+    layer_outputs, input_grads, g_qkv, g_out, g_up, g_down, g_norm = outs
+    own_norm = lax.dynamic_slice(g_norm, (0, place * block), (8, block))
+    return (
+        layer_outputs[None],
+        input_grads[None],
+        g_qkv.reshape(1, block, 3, local),
+        g_out.T[None],
+        g_up[None],
+        g_down.T[None],
+        own_norm[None, 0:2],
+        own_norm[None, 2:4],
+    )
+
+
 def solution(mesh):
     placed = (
         P("dp", None, None),
@@ -271,8 +1157,10 @@
         P("section", None, "dp"),
         P("section", None, "dp"),
     )
+    block = WIDTH // mesh.shape["dp"]
+    whole_tiles = block * mesh.shape["dp"] == WIDTH and block % 16 == 0
     return jax.shard_map(
-        shards,
+        kernel_shards if whole_tiles else shards,
         mesh=mesh,
         in_specs=placed,
         out_specs=(

time: 819 us -> 302 us (0.37)
  waiting for transfers between devices: 506 us -> 0 us
  Pallas kernels: 0 us -> 286 us
  matrix products: 102 us -> 0 us
  blocking collectives: 96 us -> 0 us
  other arithmetic: 38.9 us -> 1.37 us
  local copies, waits for them, and re-layouts: 42.7 us -> 13.3 us
  between operations: 15.5 us -> 0.7 us
  starting transfers between devices: 10.9 us -> 0 us
    pallas_call x0 -> x1, Pallas kernels: none -> 286 us  [fused(): pl.pallas_call(functools.partial(kernel, sizes), out_shape=[jax.ShapeDtyp...]
    unnamed x13 -> x0, waiting for transfers between devices: 184 us -> none
    reduce_scatter x2 -> x0, waiting for transfers between devices: 136 us -> none  [summed(): lax.psum_scatter(both.astype(first.dtype), 'dp', scatter_dimension=axis,...]
    ppermute x22 -> x0, waiting for transfers between devices: 114 us -> none  [swapped(): return lax.ppermute(value, axis, [(i, size - 1 - i) for i in range(size)])]
    dot_general x36 -> x0, matrix products: 102 us -> none  [the longest x2 19.6 us: layer_forward(): pre = jnp.dot(hidden_low, w_up, preferred_element_type=jnp.float32)]
    all_gather x3 -> x0, blocking collectives: 96 us -> none  [gathered(): own = lax.all_gather(shard[0], 'dp', axis=axis, tiled=True)]
    all_gather x3 -> x0, waiting for transfers between devices: 71.9 us -> none  [gathered(): own = lax.all_gather(shard[0], 'dp', axis=axis, tiled=True)]
    unnamed x226 -> x22, local copies, waits for them, and re-layouts: 23.6 us -> 8.71 us
  transfers between devices with their start and end apart: 31 -> 0, of which waited for: 18 -> 0; matrix products, arithmetic and copies ran while one was open for 10% -> 0% of each run, Pallas kernels for 0% -> 0%
where the time goes in v2:
time: 302 us; the launch traced here: 301 us
  Pallas kernels  286 us (95%)
  local copies, waits for them, and re-layouts  13.3 us (4%)
    pallas_call x1, Pallas kernels, fused(): pl.pallas_call(functools.partial(kernel, sizes), out_shape=[jax.ShapeDtyp...  286 us
    unnamed x22, local copies, waits for them, and re-layouts  8.71 us

profile of v2, /device:TPU:0, one launch (start us, length us, event | category | flops | bytes accessed | tf_op | source)
XLA Modules:
  0.0 301.2 jit_solution(3139621542035047531)
XLA Ops:
  0.6 0.0 copy-start
  0.7 0.7 copy-done
  1.3 0.7 fusion
  2.0 0.1 select_reduce_fusion
  2.1 0.6 pad_add_fusion.groups_ref
  2.7 0.9 broadcast_in_dim.50.keys_ref
  3.6 0.7 maximum_convert_fusion
  4.3 0.4 dynamic_update_slice.3.sn
  4.7 0.0 copy-start.6
  4.7 1.1 copy.22
  5.8 0.7 copy.24
  6.5 0.0 copy-done.6
  6.5 285.8 %shard_map.161 = (bf16[2,512,768]{2,1,0:T(8,128)(2,1)}, bf16[2,512,768]{2,1,0:T(8,128)(2,1)}, f32[96,1152]{1,0:T(8,128)}, f32[96,384]{1,0:T(8,128)}, f32[96,1536...) custom-call(bf16[2,512,768]{2,1,0:T(8,128)(2,1)} %x_ref.1, bf16[2,512,768]{2,1,0:T(8,128)(2,1)} %go_ref.1, ...), custom_call_target="tpu_custom_call" | custom-call | tf_op jit(solution)/shard_map/pallas_call | solution.py:1093
  292.3 0.0 copy-start.2
  292.3 0.9 constant_dynamic-slice_fusion
  293.2 0.6 slice_bitcast_fusion
  293.8 1.2 reshape.21
  295.0 0.8 copy.23
  295.8 0.0 copy-done.2
  295.8 0.0 copy-start.1
  295.8 1.1 copy.31
  296.9 0.8 copy-done.1
  297.8 0.0 copy-start.5
  297.8 0.0 copy-start.4
  297.8 0.0 copy-start.3
  297.8 1.1 copy.32
  298.9 0.0 copy-done.5
  298.9 0.7 copy.33
  299.6 0.0 copy-done.4
  299.6 0.8 copy.34
  300.4 0.0 copy-done.3
  300.4 0.8 copy.35
  (2 shorter events, 0.0 us)
Async XLA Ops:
  0.6 0.7 copy-start
  4.7 1.8 copy-start.6
  292.3 3.5 %copy-start.2 = (bf16[2,512,768]{2,1,0:T(8,128)(2,1)S(1)}, bf16[2,512,768]{2,1,0:T(8,128)(2,1)}, u32[]{:S(2)}) copy-start(bf16[2,512,768]{2,1,0:T(8,128)(2,1)} %get-tuple-element.15) | copy-start | bytes 4718596
  295.8 2.0 copy-start.1
  297.8 1.2 copy-start.5
  297.8 1.8 copy-start.4
  297.8 2.6 copy-start.3

commit v3 on v2

--- a/solution.py
+++ b/solution.py
@@ -269,6 +269,8 @@
 CHUNK = 256
 SUB = 32
 LANES = 128
+QK, V, O, UA, UB, DA, DB, N = range(8)
+PIECES = N
 NT = (((1,), (1,)), ((), ()))
 
 
@@ -302,67 +304,57 @@
     ou,
     od,
     on,
-    wq,
-    wo,
-    wu,
-    wd,
-    wn,
-    rq,
-    ro,
-    ru,
-    rd,
-    yq,
-    yo,
-    yu,
-    yd,
-    vq,
-    vo,
-    vu,
-    vd,
-    rn,
-    yn,
-    vn,
-    ng,
-    zin,
-    packed,
-    prob,
-    mixed,
-    norm1,
-    inv1,
-    hid,
-    act,
-    slope,
-    norm2,
-    inv2,
-    gsum,
-    gtok,
-    gmix,
-    turned,
-    gtop,
-    gin,
-    work,
-    norms,
-    xs,
-    xr,
-    local_sem,
-    out_send,
-    out_recv,
-    xs_sem,
-    xr_sem,
-    az_s,
-    az_r,
-    ay_s,
-    ay_r,
-    ac_s,
-    ac_r,
-    gc_s,
-    gc_r,
-    gy_s,
-    gy_r,
-    gz_s,
-    gz_r,
+    *refs,
 ):
     nz, ny, length, width, local, units, eps, scale = sizes
+    full, refs = refs[: PIECES + 1], refs[PIECES + 1 :]
+    summed, refs = refs[:PIECES], refs[PIECES:]
+    from_y, refs = refs[:PIECES], refs[PIECES:]
+    from_z, refs = refs[:PIECES], refs[PIECES:]
+    (
+        rn,
+        yn,
+        vn,
+        ng,
+        zin,
+        packed,
+        prob,
+        mixed,
+        norm1,
+        inv1,
+        hid,
+        act,
+        slope,
+        norm2,
+        inv2,
+        gsum,
+        gtok,
+        gmix,
+        turned,
+        gtop,
+        gin,
+        work,
+        norms,
+        xs,
+        xr,
+        local_sem,
+        out_send,
+        out_recv,
+        xs_sem,
+        xr_sem,
+        az_s,
+        az_r,
+        ay_s,
+        ay_r,
+        ac_s,
+        ac_r,
+        gc_s,
+        gc_r,
+        gy_s,
+        gy_r,
+        gz_s,
+        gz_r,
+    ) = refs
     chunks = length // CHUNK
     core = lax.axis_index("section")
     place = lax.axis_index("dp")
@@ -379,12 +371,15 @@
     def to_z(k):
         return {"dp": turn(k) * ny + y}
 
-    shard = (sq, so, su, sd, sn)
-    full = (wq, wo, wu, wd, wn)
-    summed = (rq, ro, ru, rd)
-    from_y = (yq, yo, yu, yd)
-    from_z = (vq, vo, vu, vd)
-    result = (oq, oo, ou, od)
+    def pieces(q, o, u, d):
+        low, high = slice(0, units // 2), slice(units // 2, units)
+        ends = slice(0, 2 * local), slice(2 * local, 3 * local)
+        cuts = ((q, ends[0]), (q, ends[1]), (o, slice(0, local)))
+        cuts += ((u, low), (u, high), (d, low), (d, high))
+        return tuple(ref.at[:, cut] for ref, cut in cuts)
+
+    shard = pieces(sq, so, su, sd) + (sn,)
+    result = pieces(oq, oo, ou, od)
 
     def remote(src, dst, send, recv, target):
         return pltpu.make_async_remote_copy(
@@ -416,29 +411,40 @@
             ref if src is None else src, ref, ac_s.at[m, slot], ac_r.at[m, slot], to_core
         )
 
-    def gather_start(l, *mats):
+    def gather_own(l, *mats):
+        @pl.when(core == l)
+        def _():
+            for m in mats:
+                gather_y(l, m, 0, shard[m]).start()
+                gather_core(l, m, 0, y, shard[m]).start()
+                full[m][l, z, y] = shard[m][...]
+
+    def gather_far(l, *mats):
         @pl.when(core == l)
         def _():
             for m in mats:
                 for k in range(1, nz):
                     gather_z(l, m, k).start()
-                gather_y(l, m, 0, shard[m]).start()
-                gather_core(l, m, 0, y, shard[m]).start()
-                full[m][l, z, y] = shard[m][...]
 
     def gather_pass(l, *mats):
         @pl.when(core == l)
         def _():
             for m in mats:
 
-                def one(k):
+                def one(k, none):
                     gather_z(l, m, k).wait_recv()
                     gather_y(l, m, k).start()
                     gather_core(l, m, k, y).start()
-
-                lax.fori_loop(1, nz, lambda k, none: (one(k), none)[1], 0)
-
-    def gather_end(l, *mats):
+                    return none
+
+                lax.fori_loop(1, nz, one, 0)
+
+    def gather_near(l, m):
+        @pl.when(core != l)
+        def _():
+            each(nz, lambda k: gather_core(l, m, k, y).wait_recv())
+
+    def gather_end(l, *mats, near=True):
         @pl.when(core == l)
         def _():
             for m in mats:
@@ -449,15 +455,14 @@
 
                 each(nz, one)
 
+        for m in mats:
+            if near:
+                gather_near(l, m)
+
         @pl.when(core != l)
         def _():
             for m in mats:
-
-                def one(k):
-                    gather_core(l, m, k, y).wait_recv()
-                    gather_core(l, m, k, other_y).wait_recv()
-
-                each(nz, one)
+                each(nz, lambda k: gather_core(l, m, k, other_y).wait_recv())
 
     def gather_drain(l, m):
         @pl.when(core == l)
@@ -556,14 +561,14 @@
 
 
     def vec_core(l):
-        return remote(ng.at[l], rn, gc_s.at[4, 0], gc_r.at[4, 0], to_core)
+        return remote(ng.at[l], rn, gc_s.at[PIECES, 0], gc_r.at[PIECES, 0], to_core)
 
     def vec_y(l):
-        return remote(ng.at[2], yn, gy_s.at[4, 0], gy_r.at[4, 0], to_y)
+        return remote(ng.at[2], yn, gy_s.at[PIECES, 0], gy_r.at[PIECES, 0], to_y)
 
     def vec_z(l, k):
         return remote(
-            ng.at[3], vn.at[k - 1], gz_s.at[4, k - 1], gz_r.at[4, k - 1], to_z(k)
+            ng.at[3], vn.at[k - 1], gz_s.at[PIECES, k - 1], gz_r.at[PIECES, k - 1], to_z(k)
         )
 
     def vec_start(l):
@@ -667,14 +672,8 @@
 
     def project(l, c):
         rows = chunk_rows(c)
-
-        def one(j):
-            cols = columns(j, local)
-            packed[l, rows, cols] = dot(
-                zin[l, rows], flat_rows(wq[l, :, :, :, cols])
-            ).astype(BF)
-
-        each(3, one)
+        for m, span in ((QK, slice(0, 2 * local)), (V, slice(2 * local, 3 * local))):
+            packed[l, rows, span] = dot(zin[l, rows], flat_rows(full[m][l])).astype(BF)
 
     low_lane = lax.broadcasted_iota(jnp.int32, (1, LANES), 1) < LANES // 2
 
@@ -685,7 +684,8 @@
     def attend(l, c):
         rows = chunk_rows(c)
         lanes = columns(c, CHUNK)
-        allowed = keys_ref[...] == groups_ref[pl.ds(l, 1), lanes]
+        keys = jnp.concatenate([keys_ref[...]] * (CHUNK // LANES), 1)
+        allowed = keys == groups_ref[pl.ds(l, 1), lanes]
 
         def one(j):
             query = packed[l, rows, columns(j, LANES)]
@@ -705,25 +705,22 @@
 
         each(local // LANES, one)
 
-    def send_product(i, c, left, right):
+    def send_product(i, l, c, *pairs):
         def one(j):
-            span = width // 2
-            xs[c, :, columns(j, span)] = dot_nt(left(), right(j)).astype(BF)
+            total = 0.0
+            for left, m in pairs:
+                right = flat_rows(full[m][l, pl.ds(j * (nz // 2), nz // 2)])
+                total = total + dot_nt(left(), right)
+            xs[c, :, columns(j, width // 2)] = total.astype(BF)
 
         each(2, one)
         send(i, c)
 
-    def half_rows(ref, l, j):
-        return flat_rows(ref[l, pl.ds(j * (nz // 2), nz // 2)])
-
     def attend_out(i, l, c):
-        attend(l, c)
-        send_product(
-            i, c, lambda: mixed[l, chunk_rows(c)], lambda j: half_rows(wo, l, j)
-        )
+        send_product(i, l, c, (lambda: mixed[l, chunk_rows(c)], O))
 
     def gather_norms(l):
-        norms[l] = jnp.sum(flat_rows(wn[l]).reshape(nz * ny, 8, width), 0)
+        norms[l] = jnp.sum(flat_rows(full[PIECES][l]).reshape(nz * ny, 8, width), 0)
 
     def norm_of(l, which):
         return norms[l, which : which + 1], norms[l, 2 + which : 3 + which]
@@ -747,10 +744,9 @@
 
         each(CHUNK // SUB, one)
 
-        def tile(j):
-            span = units // 3
-            cols = columns(j, span)
-            work[...] = dot(hid[l, rows], flat_rows(wu[l, :, :, :, cols]))
+        def tile(m):
+            cols = slice((m - UA) * units // 2, (m - UA + 1) * units // 2)
+            work[...] = dot(hid[l, rows], flat_rows(full[m][l]))
 
             def piece(r):
                 sub = sub_rows(c, r)
@@ -762,8 +758,16 @@
 
             each(CHUNK // SUB, piece)
 
-        each(3, tile)
-        send_product(i + 1, c, lambda: act[l, rows], lambda j: half_rows(wd, l, j))
+        tile(UA)
+        tile(UB)
+
+    def halves(ref, l, rows):
+        low, high = slice(0, units // 2), slice(units // 2, units)
+        return (lambda: ref[l, rows, low]), (lambda: ref[l, rows, high])
+
+    def contract(i, l, c):
+        low, high = halves(act, l, chunk_rows(c))
+        send_product(i, l, c, (low, DA), (high, DB))
 
     def second_norm(i, l, c, r):
         sub = sub_rows(c, r)
@@ -793,36 +797,36 @@
 
     def expand_back(i, l, c):
         rows = chunk_rows(c)
-
-        def tile(j):
-            span = units // 3
-            cols = columns(j, span)
-            grad = dot(gtok[rows], flat_rows(wd[l, :, :, :, cols]))
+        for m in (DA, DB):
+            cols = slice((m - DA) * units // 2, (m - DA + 1) * units // 2)
+            grad = dot(gtok[rows], flat_rows(full[m][l]))
             slope[l, rows, cols] = (grad * slope[l, rows, cols].astype(F32)).astype(BF)
 
-        each(3, tile)
-        send_product(i, c, lambda: slope[l, rows], lambda j: half_rows(wu, l, j))
-
-    def weight_grad(l, m, source, right, span):
-        gather_drain(l, m)
+        low, high = halves(slope, l, rows)
+        send_product(i, l, c, (low, UA), (high, UB))
+
+    def flip(source):
         step = length // 4
 
-        def flip(j):
+        def one(j):
             rows = pl.ds(pl.multiple_of(j * step, step), step)
             turned[:, columns(j, step)] = source[rows].astype(F32).T.astype(BF)
 
-        each(4, flip)
+        each(4, one)
+
+    def weight_grad(l, m, right, start=0):
+        gather_drain(l, m)
 
         def tile(j):
-            cols = columns(j, span)
+            cols = pl.ds(pl.multiple_of(start + j * local, LANES), local)
             for part in range(2):
                 rows = slice(part * width // 2, (part + 1) * width // 2)
-                grad = dot(turned[rows], right(cols)).astype(BF)
-                full[m][l, part * nz // 2 : (part + 1) * nz // 2, :, :, cols] = grad.reshape(
-                    nz // 2, ny, width // (nz * ny), span
-                )
-
-        each(full[m].shape[-1] // span, tile)
+                grad = dot(turned[rows], right[l, :, cols]).astype(BF)
+                full[m][
+                    l, part * nz // 2 : (part + 1) * nz // 2, :, :, columns(j, local)
+                ] = grad.reshape(nz // 2, ny, width // (nz * ny), local)
+
+        each(full[m].shape[-1] // local, tile)
         sum_start(l, m)
 
     def attend_back(l):
@@ -863,11 +867,16 @@
             gtok[sub] = back.astype(BF)
 
         each(CHUNK // SUB, one)
-        gmix[rows] = dot(gtok[rows], flat_rows(wo[l])).astype(BF)
+        gmix[rows] = dot(gtok[rows], flat_rows(full[O][l])).astype(BF)
 
     def project_back(i, l, c):
+        rows = chunk_rows(c)
         send_product(
-            i, c, lambda: packed[l, chunk_rows(c)], lambda j: half_rows(wq, l, j)
+            i,
+            l,
+            c,
+            (lambda: packed[l, rows, 0 : 2 * local], QK),
+            (lambda: packed[l, rows, 2 * local : 3 * local], V),
         )
 
 
@@ -882,31 +891,37 @@
     ng[...] = jnp.zeros_like(ng)
     pl.semaphore_wait(barrier, len(peers))
 
-    Q, O, U, D, N = range(5)
-    gather_start(0, Q, N)
-    gather_start(0, O)
-    gather_pass(0, Q, N)
-    gather_start(0, U)
-    gather_end(0, Q, N)
+    gather_own(0, QK, V, N, O, UA, UB, DA, DB)
+    gather_far(0, QK, V, N, O)
+    gather_pass(0, QK, V, N)
+    gather_far(0, UA)
+    gather_pass(0, O)
+    gather_end(0, QK, V, N)
+    gather_own(1, QK, V, N, O, UA, UB, DA, DB)
     first_rows.wait()
     gather_norms(0)
     each(chunks, lambda c: project(0, c))
-    gather_pass(0, O)
+    gather_far(0, UB)
+    attend(0, 0)
+    gather_pass(0, UA)
+    gather_far(0, DA)
     gather_end(0, O)
-    each(chunks, lambda c: attend_out(0, 0, c))
-    gather_pass(0, U)
-    gather_start(0, D)
-    gather_end(0, U)
-    gather_start(1, Q, N)
-    gather_pass(0, D)
-    gather_end(0, D)
-    gather_start(1, O)
-    gather_start(1, U)
-    each(chunks, lambda c: expand(0, 0, c))
-
-    gather_pass(1, Q, N)
-    gather_end(1, Q, N)
-    gather_norms(1)
+    attend_out(0, 0, 0)
+    attend(0, 1)
+    attend_out(0, 0, 1)
+    gather_pass(0, UB)
+    gather_far(0, DB)
+    gather_end(0, UA, UB)
+    gather_pass(0, DA)
+    expand(0, 0, 0)
+    gather_pass(0, DB)
+    gather_near(0, DB)
+    gather_far(1, QK, V, N, O)
+    expand(0, 0, 1)
+    gather_end(0, DA)
+    gather_end(0, DB, near=False)
+    gather_far(1, UA)
+    each(chunks, lambda c: contract(1, 0, c))
 
     def into_second(c):
         arrive(1, c)
@@ -920,19 +935,32 @@
             zin[1, sub] = (normed * gain + shift).astype(BF)
 
         each(CHUNK // SUB, one)
-        project(1, c)
-
-    each(chunks, into_second)
+
+    into_second(0)
+    gather_pass(1, QK, V, N, O)
+    gather_far(1, UB)
+    gather_pass(1, UA)
+    gather_far(1, DA)
+    into_second(1)
     out_start(0, 0, zin.at[1], lo_ref)
-    gather_pass(1, O)
-    gather_start(1, D)
+    gather_end(1, QK, V, N)
+    gather_norms(1)
+    each(chunks, lambda c: project(1, c))
+    gather_pass(1, UB)
+    gather_far(1, DB)
+    attend(1, 0)
     gather_end(1, O)
-    each(chunks, lambda c: attend_out(2, 1, c))
-    gather_pass(1, U)
-    gather_end(1, U)
-    gather_pass(1, D)
-    gather_end(1, D)
-    each(chunks, lambda c: expand(2, 1, c))
+    attend_out(2, 1, 0)
+    attend(1, 1)
+    attend_out(2, 1, 1)
+    gather_pass(1, DA)
+    gather_end(1, UA, UB)
+    expand(2, 1, 0)
+    gather_pass(1, DB)
+    gather_end(1, DA, DB)
+    contract(3, 1, 0)
+    expand(2, 1, 1)
+    contract(3, 1, 1)
     top_rows.wait()
 
     def over_top(c):
@@ -946,21 +974,33 @@
             gtop[sub] = (normed * gain + shift).astype(BF)
 
         each(CHUNK // SUB, one)
-        expand_back(4, 1, c)
-
-    each(chunks, over_top)
+
+    over_top(0)
+    expand_back(4, 1, 0)
+    over_top(1)
+    expand_back(4, 1, 1)
     out_start(1, 1, gtop, lo_ref)
-    third = units // 3
-    weight_grad(1, D, gtok, lambda cols: act[1, :, cols], third)
-    weight_grad(1, U, hid.at[1], lambda cols: slope[1, :, cols], third)
-    each(chunks, lambda c: middle_back(4, 1, c))
-    weight_grad(1, O, gtok, lambda cols: mixed[1, :, cols], local)
+    flip(gtok)
+    weight_grad(1, DA, act)
+    weight_grad(1, DB, act, units // 2)
+    flip(hid.at[1])
+    weight_grad(1, UA, slope)
+    weight_grad(1, UB, slope, units // 2)
+    middle_back(4, 1, 0)
+    sum_first(1, DA)
+    middle_back(4, 1, 1)
+    sum_first(1, DB)
     attend_back(1)
     each(chunks, lambda c: project_back(5, 1, c))
-    weight_grad(1, Q, zin.at[1], lambda cols: packed[1, :, cols], local)
+    sum_first(1, UA)
+    flip(gtok)
+    weight_grad(1, O, mixed)
+    flip(zin.at[1])
+    weight_grad(1, QK, packed)
+    weight_grad(1, V, packed, 2 * local)
     vec_start(1)
-    sum_first(1, D)
-    sum_first(1, U)
+    sum_second(1, DA)
+    sum_first(1, UB)
 
     def under(c):
         arrive(5, c)
@@ -974,34 +1014,47 @@
         each(CHUNK // SUB, one)
         expand_back(6, 0, c)
 
-    each(chunks, under)
+    under(0)
+    sum_second(1, DB)
+    sum_first(1, O)
+    sum_first(1, QK)
+    sum_second(1, UA)
+    under(1)
     out_start(1, 3, gin, ig_ref)
-    weight_grad(0, D, gtok, lambda cols: act[0, :, cols], third)
-    weight_grad(0, U, hid.at[0], lambda cols: slope[0, :, cols], third)
-    sum_second(1, D)
-    sum_second(1, U)
-    sum_first(1, O)
-    sum_first(1, Q)
+    flip(gtok)
+    weight_grad(0, DA, act)
+    weight_grad(0, DB, act, units // 2)
+    flip(hid.at[0])
+    weight_grad(0, UA, slope)
+    weight_grad(0, UB, slope, units // 2)
+    sum_first(1, V)
     vec_first(1)
-    each(chunks, lambda c: middle_back(6, 0, c))
-    weight_grad(0, O, gtok, lambda cols: mixed[0, :, cols], local)
-    sum_first(0, D)
-    sum_first(0, U)
-    sum_first(0, O)
+    sum_second(1, UB)
+    middle_back(6, 0, 0)
+    sum_first(0, DA)
+    middle_back(6, 0, 1)
+    sum_first(0, DB)
+    sum_second(1, O)
+    sum_second(1, QK)
     attend_back(0)
     each(chunks, lambda c: project_back(7, 0, c))
-    weight_grad(0, Q, zin.at[0], lambda cols: packed[0, :, cols], local)
+    sum_first(0, UA)
+    sum_second(0, DA)
+    flip(gtok)
+    weight_grad(0, O, mixed)
+    flip(zin.at[0])
+    weight_grad(0, QK, packed)
+    weight_grad(0, V, packed, 2 * local)
     vec_start(0)
-    sum_second(1, O)
-    sum_second(1, Q)
+    sum_first(0, UB)
+    sum_second(0, DB)
+    sum_second(1, V)
     vec_second(1)
-    sum_last(1, D)
-    sum_last(1, U)
-    sum_second(0, D)
-    sum_first(0, Q)
+    sum_first(0, O)
+    sum_first(0, QK)
+    sum_first(0, V)
     vec_first(0)
-    sum_second(0, U)
-    sum_second(0, O)
+    sum_second(0, UA)
 
     def bottom(c):
         arrive(7, c)
@@ -1013,17 +1066,20 @@
         each(CHUNK // SUB, one)
 
     out_wait(1, 1, gtop, lo_ref)
-    each(chunks, bottom)
+    bottom(0)
+    sum_second(0, UB)
+    bottom(1)
     out_start(0, 2, gtop, ig_ref)
-    sum_second(0, Q)
+    sum_second(0, O)
+    sum_second(0, QK)
+    sum_second(0, V)
     vec_second(0)
     for l in (1, 0):
-        for m in (D, U, O, Q):
-            if l == 0 or m in (O, Q):
-                sum_last(l, m)
+        for m in (DA, DB, UA, UB, O, QK, V):
+            sum_last(l, m)
         vec_last(l)
     for l in range(2):
-        for m in (Q, O, U, D):
+        for m in range(PIECES):
             sum_drain(l, m)
         vec_drain(l)
         gather_drain(l, N)
@@ -1036,7 +1092,8 @@
     nz, ny, length, width, local, units, eps, scale = sizes
     block = width // (nz * ny)
     chunks = length // CHUNK
-    spans = (3 * local, local, units, units)
+    spans = (2 * local, local, local) + (units // 2,) * 4
+    outs = (3 * local, local, units, units)
     dma = pltpu.SemaphoreType.DMA
     vmem = pltpu.VMEM
     scratch = [vmem((2, nz, ny, block, span), BF) for span in spans]
@@ -1066,7 +1123,7 @@
         vmem((width, length), BF),
         vmem((length, width), BF),
         vmem((length, width), BF),
-        vmem((CHUNK, units // 3), F32),
+        vmem((CHUNK, units // 2), F32),
         vmem((2, 8, width), F32),
         vmem((chunks, CHUNK, width), BF),
         vmem((2, chunks, CHUNK, width), BF),
@@ -1075,25 +1132,25 @@
         dma((4,)),
         dma((chunks,)),
         dma((2, chunks)),
-        dma((5, nz - 1)),
-        dma((5, nz - 1)),
-        dma((5, nz)),
-        dma((5, nz)),
-        dma((5, 2 * nz)),
-        dma((5, 2 * nz)),
-        dma((5, 2)),
-        dma((5, 2)),
-        dma((5, nz)),
-        dma((5, nz)),
-        dma((5, nz - 1)),
-        dma((5, nz - 1)),
+        dma((PIECES + 1, nz - 1)),
+        dma((PIECES + 1, nz - 1)),
+        dma((PIECES + 1, nz)),
+        dma((PIECES + 1, nz)),
+        dma((PIECES + 1, 2 * nz)),
+        dma((PIECES + 1, 2 * nz)),
+        dma((PIECES + 1, 2)),
+        dma((PIECES + 1, 2)),
+        dma((PIECES + 1, nz)),
+        dma((PIECES + 1, nz)),
+        dma((PIECES + 1, nz - 1)),
+        dma((PIECES + 1, nz - 1)),
     ]
     anywhere = pl.BlockSpec(memory_space=pl.ANY)
     inside = pl.BlockSpec(memory_space=pltpu.VMEM)
     return pl.pallas_call(
         functools.partial(kernel, sizes),
         out_shape=[jax.ShapeDtypeStruct((2, length, width), BF)] * 2
-        + [jax.ShapeDtypeStruct((block, span), F32) for span in spans]
+        + [jax.ShapeDtypeStruct((block, span), F32) for span in outs]
         + [jax.ShapeDtypeStruct((8, width), F32)],
         in_specs=[anywhere] * 2 + [inside] * 7,
         out_specs=[anywhere] * 2 + [inside] * 5,
@@ -1116,7 +1173,7 @@
     sizes = (parts // 2, 2, length, width, local, units, norm_eps, score_scale)
     own = lax.dynamic_index_in_dim(segments, core, 0, False)
     mapped = partner_of(own, lax.dynamic_index_in_dim(partner, core, 0, False))
-    keys = jnp.broadcast_to(own[:, None], (length, CHUNK))
+    keys = jnp.broadcast_to(own[:, None], (length, LANES))
     groups = jnp.stack([own, mapped])
     vectors = jnp.concatenate([norm_gain[0], norm_shift[0]]).astype(F32)
     spread = lax.dynamic_update_slice(

time: 302 us -> 263 us (0.87)
  Pallas kernels: 286 us -> 247 us
    pallas_call x1, Pallas kernels: 286 us -> 247 us  [fused(): pl.pallas_call(functools.partial(kernel, sizes), out_shape=[jax.ShapeDtyp...]
where the time goes in v3:
time: 263 us; the launch traced here: 262 us
  Pallas kernels  247 us (94%)
  local copies, waits for them, and re-layouts  13.3 us (5%)
    pallas_call x1, Pallas kernels, fused(): pl.pallas_call(functools.partial(kernel, sizes), out_shape=[jax.ShapeDtyp...  247 us
    unnamed x22, local copies, waits for them, and re-layouts  8.71 us

profile of v3, /device:TPU:0, one launch (start us, length us, event | category | flops | bytes accessed | tf_op | source)
XLA Modules:
  0.0 262.4 jit_solution(9467475361077303970)
XLA Ops:
  0.6 0.0 copy-start
  0.7 0.7 copy-done
  1.3 0.7 fusion
  2.0 0.1 select_reduce_fusion
  2.1 0.6 pad_add_fusion.groups_ref
  2.7 0.8 broadcast_in_dim.50.keys_ref
  3.5 0.7 maximum_convert_fusion
  4.2 0.4 dynamic_update_slice.3.sn
  4.6 0.0 copy-start.6
  4.6 1.1 copy.22
  5.7 0.7 copy.24
  6.4 0.0 copy-done.6
  6.4 247.1 %shard_map.161 = (bf16[2,512,768]{2,1,0:T(8,128)(2,1)}, bf16[2,512,768]{2,1,0:T(8,128)(2,1)}, f32[96,1152]{1,0:T(8,128)}, f32[96,384]{1,0:T(8,128)}, f32[96,1536...) custom-call(bf16[2,512,768]{2,1,0:T(8,128)(2,1)} %x_ref.1, bf16[2,512,768]{2,1,0:T(8,128)(2,1)} %go_ref.1, ...), custom_call_target="tpu_custom_call" | custom-call | tf_op jit(solution)/shard_map/pallas_call | solution.py:1150
  253.5 0.0 copy-start.2
  253.5 0.9 constant_dynamic-slice_fusion
  254.4 0.6 slice_bitcast_fusion
  255.0 1.2 reshape.21
  256.2 0.8 copy.23
  257.0 0.0 copy-done.2
  257.0 0.0 copy-start.1
  257.0 1.1 copy.31
  258.1 0.8 copy-done.1
  258.9 0.0 copy-start.5
  258.9 0.0 copy-start.4
  258.9 0.0 copy-start.3
  259.0 1.1 copy.32
  260.1 0.0 copy-done.5
  260.1 0.7 copy.33
  260.8 0.0 copy-done.4
  260.8 0.8 copy.34
  261.6 0.0 copy-done.3
  261.6 0.8 copy.35
  (2 shorter events, 0.0 us)
Async XLA Ops:
  0.6 0.7 copy-start
  4.6 1.8 copy-start.6
  253.5 3.5 %copy-start.2 = (bf16[2,512,768]{2,1,0:T(8,128)(2,1)S(1)}, bf16[2,512,768]{2,1,0:T(8,128)(2,1)}, u32[]{:S(2)}) copy-start(bf16[2,512,768]{2,1,0:T(8,128)(2,1)} %get-tuple-element.15) | copy-start | bytes 4718596
  257.0 2.0 copy-start.1
  258.9 1.2 copy-start.5
  258.9 1.8 copy-start.4
  258.9 2.6 %copy-start.3 = (f32[96,1536]{1,0:T(8,128)S(1)}, f32[96,1536]{1,0:T(8,128)}, u32[]{:S(2)}) copy-start(f32[96,1536]{1,0:T(8,128)} %get-tuple-element.20) | copy-start | bytes 1769476
